TPU v7x, 128 devices: a whole 4x4x4 slice. The times are simulated.
128 devices in a mesh: row: 32 (over y, z_lo, x), col: 4 (over z_hi, core).
Axes of the slice: x: 4, y: 4, z: 4 (z_hi: 2, z_lo: 2; z = z_hi * 2 + z_lo), core: 2. Of those that a mesh axis runs over, the one named last changes fastest.
Arguments:
- pair_map: bfloat16 [1536, 1536, 128], P('row', 'col'), may hold values from -6 to 6
- valid_tokens: int32 [1536], replicated, may hold values from 0 to 1, as said below
- ln_gain: float32 [128], replicated, may hold values from 0.1 to 1.9
- ln_bias: float32 [128], replicated, may hold values from -3 to 3
- w_bias: bfloat16 [128, 4], replicated, may hold values from -0.5 to 0.5
- w_query: bfloat16 [128, 128], replicated, may hold values from -4.6 to 4.6
- w_key: bfloat16 [128, 128], replicated, may hold values from -4.6 to 4.6
- w_value: bfloat16 [128, 128], replicated, may hold values from -0.5 to 0.5
- w_gate: bfloat16 [128, 128], replicated, may hold values from -0.5 to 0.5
- gate_bias: float32 [128], replicated, may hold values from -4 to 4
- w_out: bfloat16 [128, 128], replicated, may hold values from -0.5 to 0.5
Outputs:
- update: bfloat16 [1536, 1536, 128], P('row', 'col')
Inputs may be any that keep to these rules, and one draw needn't show every extreme that they name: `valid_tokens`: the residues form 4 chains of 384 positions each; in each chain the real residues come first, at least 192 of them, then padding.
All inputs are finite; a program needn't handle non-finite values.
Results may differ from a plain program's by a relative error of at most 0.014.
The roundings to bfloat16 on the way count: a program that leaves them out, or rounds other values in their place, can miss the bound.
Values may be sent and summed in bfloat16 or wider, within the bound.
A program may use at most 256 MiB of HBM per device.

v0:
```python
import math

import jax
import jax.numpy as jnp
from jax import lax
from jax.sharding import PartitionSpec as P


def normalize(pair_map, ln_gain, ln_bias):
    values_f32 = pair_map.astype(jnp.float32)
    average = jnp.mean(values_f32, axis=-1, keepdims=True)
    centered = values_f32 - average
    variance = jnp.mean(centered * centered, axis=-1, keepdims=True)
    return (centered * lax.rsqrt(variance + 1e-05) * ln_gain + ln_bias).astype(jnp.bfloat16)


def shards(
    pair_map,
    valid_tokens,
    ln_gain,
    ln_bias,
    w_bias,
    w_query,
    w_key,
    w_value,
    w_gate,
    gate_bias,
    w_out,
):
    row_count, col_count, channels = pair_map.shape
    head_count = w_bias.shape[1]
    inner_width = w_query.shape[1]
    head_width = inner_width // head_count
    normed = normalize(pair_map, ln_gain, ln_bias)
    planes = jnp.dot(
        normed.reshape(row_count * col_count, channels), w_bias, preferred_element_type=jnp.float32
    )
    planes = (
        planes.astype(jnp.bfloat16).reshape(row_count, col_count, head_count).transpose(2, 0, 1)
    )
    transposed = lax.all_to_all(normed, "row", split_axis=1, concat_axis=0, tiled=True)
    all_rows, own_cols, _ = transposed.shape
    flattened = transposed.reshape(all_rows * own_cols, channels)
    score_scale = 1.0 / math.sqrt(head_width)

    def project(weight):
        return jnp.dot(flattened, weight, preferred_element_type=jnp.float32)

    def heads_first(values_bf16):
        return values_bf16.reshape(all_rows, own_cols, head_count, head_width).transpose(1, 0, 2, 3)

    query_cols = heads_first((project(w_query) * score_scale).astype(jnp.bfloat16))
    key_cols = heads_first(project(w_key).astype(jnp.bfloat16))
    value_cols = heads_first(project(w_value).astype(jnp.bfloat16))
    gate_cols = (
        jax.nn.sigmoid(project(w_gate) + gate_bias)
        .reshape(all_rows, own_cols, inner_width)
        .transpose(1, 0, 2)
    )
    negative = (valid_tokens.astype(jnp.float32) - 1.0) * 1000000000.0

    def finish(gate_value, attended):
        hidden = (gate_value * attended.reshape(all_rows, inner_width)).astype(jnp.bfloat16)
        return jnp.dot(hidden, w_out, preferred_element_type=jnp.float32).astype(jnp.bfloat16)

    gathered_cols = lax.all_gather(planes, "col", axis=2, tiled=True)
    full_planes = lax.all_gather(gathered_cols, "row", axis=1, tiled=True)
    planes_t = jnp.swapaxes(full_planes, 1, 2)

    def column(column_data):
        query_col, key_col, value_col, gate_value = column_data
        scores = jnp.einsum("ihc,khc->hik", query_col, key_col, preferred_element_type=jnp.float32)
        scores = scores + planes_t.astype(jnp.float32) + negative
        weights = jax.nn.softmax(scores, axis=-1).astype(jnp.bfloat16)
        attended = jnp.einsum(
            "hik,khc->ihc", weights, value_col, preferred_element_type=jnp.float32
        )
        return finish(gate_value, attended)

    updates = lax.map(column, (query_cols, key_cols, value_cols, gate_cols))
    returned = jnp.swapaxes(updates, 0, 1)
    return lax.all_to_all(returned, "row", split_axis=0, concat_axis=1, tiled=True)


def solution(mesh):
    return jax.shard_map(
        shards,
        mesh=mesh,
        in_specs=(P("row", "col", None), P(), P(), P(), P(), P(), P(), P(), P(), P(), P()),
        out_specs=P("row", "col", None),
        check_vma=False,
    )
```

profile of v0, /device:TPU:0, one launch (start us, length us, event | category | flops | bytes accessed | tf_op | source)
XLA Modules:
  0.0 1114.4 jit_solution(11759911388577989120)
XLA Ops:
  62.9 94.7 %all-to-all-done = bf16[48,384,128]{2,0,1:T(8,128)(2,1)} async-done(((bf16[48,384,128]{2,0,1:T(8,128)(2,1)}), bf16[48,384,128]{2,0,1:T(8,128)(2,1)}, u32[]{:S(2)}, u32[]{:S(2)}) %all-to-all-start) | async-done | bytes 4718624 | tf_op jit(solution)/shard_map/all_to_all | solution.py:41
  179.0 24.4 %reshape.45 = bf16[1536,12,4,32]{3,2,1,0:T(4,128)(2,1)} reshape(bf16[18432,128]{1,0:T(8,128)(2,1)} %convolution_convert_fusion.2) | data formatting | bytes 9437184 | tf_op jit(solution)/shard_map/reshape | solution.py:50
  203.5 26.1 %copy.41 = bf16[12,1536,4,32]{1,3,2,0:T(8,128)(2,1)} copy(bf16[12,1536,4,32]{3,2,0,1:T(4,128)(2,1)} %bitcast.98) | data formatting | bytes 9437184 | tf_op jit(solution)/shard_map/while | solution.py:80
  235.5 24.4 %reshape.46 = bf16[1536,12,4,32]{3,2,1,0:T(4,128)(2,1)} reshape(bf16[18432,128]{1,0:T(8,128)(2,1)} %fusion.46) | data formatting | bytes 9437184 | tf_op jit(solution)/shard_map/reshape | solution.py:50
  259.9 26.1 %copy.42 = bf16[12,1536,4,32]{1,3,2,0:T(8,128)(2,1)} copy(bf16[12,1536,4,32]{3,2,0,1:T(4,128)(2,1)} %bitcast.99) | data formatting | bytes 9437184 | tf_op jit(solution)/shard_map/while | solution.py:80
  291.9 24.4 %reshape.47 = bf16[1536,12,4,32]{3,2,1,0:T(4,128)(2,1)} reshape(bf16[18432,128]{1,0:T(8,128)(2,1)} %convolution_convert_fusion.1) | data formatting | bytes 9437184 | tf_op jit(solution)/shard_map/reshape | solution.py:50
  316.3 26.0 %copy.43 = bf16[12,1536,4,32]{1,3,2,0:T(8,128)(2,1)} copy(bf16[12,1536,4,32]{3,2,0,1:T(4,128)(2,1)} %bitcast.100) | data formatting | bytes 9437184 | tf_op jit(solution)/shard_map/while | solution.py:80
  362.3 491.5 %while.10 = (s32[]{:T(128)}, bf16[12,1536,128]{2,1,0:T(8,128)(2,1)}, f32[12,1536,128]{2,0,1:T(8,128)}, bf16[12,1536,4,32]{1,3,2,0:T(8,128)(2,1)}, bf16[12,1536,4...) while((s32[]{:T(128)}, ...), condition=%wide.region_5.6_spmd, body=%wide.region_2.5_spmd.sunk | while | flops 1966679040 | bytes 46496872 | solution.py:80
  362.5 16.9 %exponential_reduce_fusion.2 = f32[4,1536]{1,0:T(4,128)S(1)} fusion(bf16[4,1536,1536]{1,2,0:T(8,128)(2,1)} %get-tuple-element.179, f32[1536]{0:T(1024)S(1)} %get-tuple-element.180, bf16[12,1536,4,32]{1,3,2,0:T(8,128)(2,1)} %get-tuple-element.178, s32[]{:T(128)} %get-tuple-element.163, bf16[12,1536,4,32]{1,3,2,0:T(8,128)(2,1)} %get-tuple-element.177), kind=kOutput, calls=%fused_computation.5.clone.1 | convolution fusion | flops 651167232 | bytes 19692544 | tf_op jit(solution)/shard_map/while/body/eval_jaxpr/sub | solution.py:74
  379.4 19.2 %fusion.87 = f32[4,32,1536]{2,1,0:T(8,128)S(1)} fusion(f32[4,1536]{1,0:T(4,128)S(1)} %exponential_reduce_fusion.2, bf16[4,1536,1536]{1,2,0:T(8,128)(2,1)} %get-tuple-element.179, f32[1536]{0:T(1024)S(1)} %get-tuple-element.180, bf16[12,1536,4,32]{1,3,2,0:T(8,128)(2,1)} %get-tuple-element.176, s32[]{:T(128)} %get-tuple-element.163, ...), kind=kOutput, calls=%fused_computation.6.clone.1 | convolution fusion | flops 1264590336 | bytes 20872704 | tf_op jit(solution)/shard_map/while/body/eval_jaxpr/hik,khc->ihc/dot_general | solution.py:75
  420.4 19.2 %fusion.87 = f32[4,32,1536]{2,1,0:T(8,128)S(1)} fusion(f32[4,1536]{1,0:T(4,128)S(1)} %exponential_reduce_fusion.2, bf16[4,1536,1536]{1,2,0:T(8,128)(2,1)} %get-tuple-element.179, f32[1536]{0:T(1024)S(1)} %get-tuple-element.180, bf16[12,1536,4,32]{1,3,2,0:T(8,128)(2,1)} %get-tuple-element.176, s32[]{:T(128)} %get-tuple-element.163, ...), kind=kOutput, calls=%fused_computation.6.clone.1 | convolution fusion | flops 1264590336 | bytes 20872704 | tf_op jit(solution)/shard_map/while/body/eval_jaxpr/hik,khc->ihc/dot_general | solution.py:75
  444.4 16.9 %exponential_reduce_fusion.2 = f32[4,1536]{1,0:T(4,128)S(1)} fusion(bf16[4,1536,1536]{1,2,0:T(8,128)(2,1)} %get-tuple-element.179, f32[1536]{0:T(1024)S(1)} %get-tuple-element.180, bf16[12,1536,4,32]{1,3,2,0:T(8,128)(2,1)} %get-tuple-element.178, s32[]{:T(128)} %get-tuple-element.163, bf16[12,1536,4,32]{1,3,2,0:T(8,128)(2,1)} %get-tuple-element.177), kind=kOutput, calls=%fused_computation.5.clone.1 | convolution fusion | flops 651167232 | bytes 19692544 | tf_op jit(solution)/shard_map/while/body/eval_jaxpr/sub | solution.py:74
  461.3 19.2 %fusion.87 = f32[4,32,1536]{2,1,0:T(8,128)S(1)} fusion(f32[4,1536]{1,0:T(4,128)S(1)} %exponential_reduce_fusion.2, bf16[4,1536,1536]{1,2,0:T(8,128)(2,1)} %get-tuple-element.179, f32[1536]{0:T(1024)S(1)} %get-tuple-element.180, bf16[12,1536,4,32]{1,3,2,0:T(8,128)(2,1)} %get-tuple-element.176, s32[]{:T(128)} %get-tuple-element.163, ...), kind=kOutput, calls=%fused_computation.6.clone.1 | convolution fusion | flops 1264590336 | bytes 20872704 | tf_op jit(solution)/shard_map/while/body/eval_jaxpr/hik,khc->ihc/dot_general | solution.py:75
  485.3 16.9 %exponential_reduce_fusion.2 = f32[4,1536]{1,0:T(4,128)S(1)} fusion(bf16[4,1536,1536]{1,2,0:T(8,128)(2,1)} %get-tuple-element.179, f32[1536]{0:T(1024)S(1)} %get-tuple-element.180, bf16[12,1536,4,32]{1,3,2,0:T(8,128)(2,1)} %get-tuple-element.178, s32[]{:T(128)} %get-tuple-element.163, bf16[12,1536,4,32]{1,3,2,0:T(8,128)(2,1)} %get-tuple-element.177), kind=kOutput, calls=%fused_computation.5.clone.1 | convolution fusion | flops 651167232 | bytes 19692544 | tf_op jit(solution)/shard_map/while/body/eval_jaxpr/sub | solution.py:74
  502.2 19.2 %fusion.87 = f32[4,32,1536]{2,1,0:T(8,128)S(1)} fusion(f32[4,1536]{1,0:T(4,128)S(1)} %exponential_reduce_fusion.2, bf16[4,1536,1536]{1,2,0:T(8,128)(2,1)} %get-tuple-element.179, f32[1536]{0:T(1024)S(1)} %get-tuple-element.180, bf16[12,1536,4,32]{1,3,2,0:T(8,128)(2,1)} %get-tuple-element.176, s32[]{:T(128)} %get-tuple-element.163, ...), kind=kOutput, calls=%fused_computation.6.clone.1 | convolution fusion | flops 1264590336 | bytes 20872704 | tf_op jit(solution)/shard_map/while/body/eval_jaxpr/hik,khc->ihc/dot_general | solution.py:75
  543.1 19.2 %fusion.87 = f32[4,32,1536]{2,1,0:T(8,128)S(1)} fusion(f32[4,1536]{1,0:T(4,128)S(1)} %exponential_reduce_fusion.2, bf16[4,1536,1536]{1,2,0:T(8,128)(2,1)} %get-tuple-element.179, f32[1536]{0:T(1024)S(1)} %get-tuple-element.180, bf16[12,1536,4,32]{1,3,2,0:T(8,128)(2,1)} %get-tuple-element.176, s32[]{:T(128)} %get-tuple-element.163, ...), kind=kOutput, calls=%fused_computation.6.clone.1 | convolution fusion | flops 1264590336 | bytes 20872704 | tf_op jit(solution)/shard_map/while/body/eval_jaxpr/hik,khc->ihc/dot_general | solution.py:75
  584.0 19.2 %fusion.87 = f32[4,32,1536]{2,1,0:T(8,128)S(1)} fusion(f32[4,1536]{1,0:T(4,128)S(1)} %exponential_reduce_fusion.2, bf16[4,1536,1536]{1,2,0:T(8,128)(2,1)} %get-tuple-element.179, f32[1536]{0:T(1024)S(1)} %get-tuple-element.180, bf16[12,1536,4,32]{1,3,2,0:T(8,128)(2,1)} %get-tuple-element.176, s32[]{:T(128)} %get-tuple-element.163, ...), kind=kOutput, calls=%fused_computation.6.clone.1 | convolution fusion | flops 1264590336 | bytes 20872704 | tf_op jit(solution)/shard_map/while/body/eval_jaxpr/hik,khc->ihc/dot_general | solution.py:75
  624.9 19.2 %fusion.87 = f32[4,32,1536]{2,1,0:T(8,128)S(1)} fusion(f32[4,1536]{1,0:T(4,128)S(1)} %exponential_reduce_fusion.2, bf16[4,1536,1536]{1,2,0:T(8,128)(2,1)} %get-tuple-element.179, f32[1536]{0:T(1024)S(1)} %get-tuple-element.180, bf16[12,1536,4,32]{1,3,2,0:T(8,128)(2,1)} %get-tuple-element.176, s32[]{:T(128)} %get-tuple-element.163, ...), kind=kOutput, calls=%fused_computation.6.clone.1 | convolution fusion | flops 1264590336 | bytes 20872704 | tf_op jit(solution)/shard_map/while/body/eval_jaxpr/hik,khc->ihc/dot_general | solution.py:75
  665.9 19.2 %fusion.87 = f32[4,32,1536]{2,1,0:T(8,128)S(1)} fusion(f32[4,1536]{1,0:T(4,128)S(1)} %exponential_reduce_fusion.2, bf16[4,1536,1536]{1,2,0:T(8,128)(2,1)} %get-tuple-element.179, f32[1536]{0:T(1024)S(1)} %get-tuple-element.180, bf16[12,1536,4,32]{1,3,2,0:T(8,128)(2,1)} %get-tuple-element.176, s32[]{:T(128)} %get-tuple-element.163, ...), kind=kOutput, calls=%fused_computation.6.clone.1 | convolution fusion | flops 1264590336 | bytes 20872704 | tf_op jit(solution)/shard_map/while/body/eval_jaxpr/hik,khc->ihc/dot_general | solution.py:75
  706.8 19.2 %fusion.87 = f32[4,32,1536]{2,1,0:T(8,128)S(1)} fusion(f32[4,1536]{1,0:T(4,128)S(1)} %exponential_reduce_fusion.2, bf16[4,1536,1536]{1,2,0:T(8,128)(2,1)} %get-tuple-element.179, f32[1536]{0:T(1024)S(1)} %get-tuple-element.180, bf16[12,1536,4,32]{1,3,2,0:T(8,128)(2,1)} %get-tuple-element.176, s32[]{:T(128)} %get-tuple-element.163, ...), kind=kOutput, calls=%fused_computation.6.clone.1 | convolution fusion | flops 1264590336 | bytes 20872704 | tf_op jit(solution)/shard_map/while/body/eval_jaxpr/hik,khc->ihc/dot_general | solution.py:75
  747.7 19.2 %fusion.87 = f32[4,32,1536]{2,1,0:T(8,128)S(1)} fusion(f32[4,1536]{1,0:T(4,128)S(1)} %exponential_reduce_fusion.2, bf16[4,1536,1536]{1,2,0:T(8,128)(2,1)} %get-tuple-element.179, f32[1536]{0:T(1024)S(1)} %get-tuple-element.180, bf16[12,1536,4,32]{1,3,2,0:T(8,128)(2,1)} %get-tuple-element.176, s32[]{:T(128)} %get-tuple-element.163, ...), kind=kOutput, calls=%fused_computation.6.clone.1 | convolution fusion | flops 1264590336 | bytes 20872704 | tf_op jit(solution)/shard_map/while/body/eval_jaxpr/hik,khc->ihc/dot_general | solution.py:75
  788.6 19.2 %fusion.87 = f32[4,32,1536]{2,1,0:T(8,128)S(1)} fusion(f32[4,1536]{1,0:T(4,128)S(1)} %exponential_reduce_fusion.2, bf16[4,1536,1536]{1,2,0:T(8,128)(2,1)} %get-tuple-element.179, f32[1536]{0:T(1024)S(1)} %get-tuple-element.180, bf16[12,1536,4,32]{1,3,2,0:T(8,128)(2,1)} %get-tuple-element.176, s32[]{:T(128)} %get-tuple-element.163, ...), kind=kOutput, calls=%fused_computation.6.clone.1 | convolution fusion | flops 1264590336 | bytes 20872704 | tf_op jit(solution)/shard_map/while/body/eval_jaxpr/hik,khc->ihc/dot_general | solution.py:75
  829.5 19.2 %fusion.87 = f32[4,32,1536]{2,1,0:T(8,128)S(1)} fusion(f32[4,1536]{1,0:T(4,128)S(1)} %exponential_reduce_fusion.2, bf16[4,1536,1536]{1,2,0:T(8,128)(2,1)} %get-tuple-element.179, f32[1536]{0:T(1024)S(1)} %get-tuple-element.180, bf16[12,1536,4,32]{1,3,2,0:T(8,128)(2,1)} %get-tuple-element.176, s32[]{:T(128)} %get-tuple-element.163, ...), kind=kOutput, calls=%fused_computation.6.clone.1 | convolution fusion | flops 1264590336 | bytes 20872704 | tf_op jit(solution)/shard_map/while/body/eval_jaxpr/hik,khc->ihc/dot_general | solution.py:75
  859.4 243.1 %all_to_all.33 = bf16[1536,12,128]{2,1,0:T(8,128)(2,1)S(1)} all-to-all(bf16[1536,12,128]{2,1,0:T(8,128)(2,1)S(1)} %bitcast.102), channel_id=1, replica_groups=mesh['row'=32,'col'=4] {'row'}, dimensions={0} | all-to-all | bytes 9437184 | tf_op jit(solution)/shard_map/all_to_all | solution.py:82
  (108 shorter events, 329.0 us)
Async XLA Ops:
  6.5 166.6 %copy-start = (bf16[128,128]{1,0:T(8,128)(2,1)S(1)}, bf16[128,128]{1,0:T(8,128)(2,1)}, u32[]{:S(2)}) copy-start(bf16[128,128]{1,0:T(8,128)(2,1)} %param.20) | copy-start | bytes 98308
  6.5 22.8 %copy-start.10 = (f32[128]{0:T(128)S(1)}, f32[128]{0:T(128)}, u32[]{:S(2)}) copy-start(f32[128]{0:T(128)} %param.15) | copy-start | bytes 1540
  6.5 22.9 %copy-start.9 = (f32[128]{0:T(128)S(1)}, f32[128]{0:T(128)}, u32[]{:S(2)}) copy-start(f32[128]{0:T(128)} %param.16) | copy-start | bytes 1540
  6.5 355.8 %all-gather.2.cloned.1.call-start = ((), (), s32[]{:S(2)}) async-start(), calls=%async_computation.2 | async-start | bytes 19464192 | tf_op jit(solution)/shard_map/all_gather | solution.py:67
  6.5 6.5 copy-start.2
  41.7 2.6 copy-start.3
  41.8 1.2 copy-start.8
  44.3 18.6 %copy-start.7 = (s32[1536]{0:T(1024)S(1)}, s32[1536]{0:T(1024)}, u32[]{:S(2)}) copy-start(s32[1536]{0:T(1024)} %param.14) | copy-start | bytes 18436
  54.8 102.8 %all-to-all-start = ((bf16[48,384,128]{2,0,1:T(8,128)(2,1)}), bf16[48,384,128]{2,0,1:T(8,128)(2,1)}, u32[]{:S(2)}, u32[]{:S(2)}) async-start(bf16[48,384,128]{2,0,1:T(8,128)(2,1)} %copy-done.3), calls=%async_computation | async-start | bytes 9437184 | tf_op jit(solution)/shard_map/all_to_all | solution.py:41
  203.5 26.1 %copy-start.5 = (bf16[128,128]{1,0:T(8,128)(2,1)S(1)}, bf16[128,128]{1,0:T(8,128)(2,1)}, u32[]{:S(2)}) copy-start(bf16[128,128]{1,0:T(8,128)(2,1)} %param.18) | copy-start | bytes 98308
  259.9 26.1 %copy-start.6 = (bf16[128,128]{1,0:T(8,128)(2,1)S(1)}, bf16[128,128]{1,0:T(8,128)(2,1)}, u32[]{:S(2)}) copy-start(bf16[128,128]{1,0:T(8,128)(2,1)} %param.19) | copy-start | bytes 98308
  316.3 26.0 %copy-start.11 = (bf16[128,128]{1,0:T(8,128)(2,1)S(1)}, bf16[128,128]{1,0:T(8,128)(2,1)}, u32[]{:S(2)}) copy-start(bf16[128,128]{1,0:T(8,128)(2,1)} %param.21) | copy-start | bytes 98308
  316.3 26.0 %copy-start.12 = (f32[128]{0:T(128)S(1)}, f32[128]{0:T(128)}, u32[]{:S(2)}) copy-start(f32[128]{0:T(128)} %param.22) | copy-start | bytes 1540
  350.9 11.5 %copy-start.4 = (bf16[128,128]{1,0:T(8,128)(2,1)S(1)}, bf16[128,128]{1,0:T(8,128)(2,1)}, u32[]{:S(2)}) copy-start(bf16[128,128]{1,0:T(8,128)(2,1)} %param.23) | copy-start | bytes 98308
  1102.5 4.6 copy-start.1
Sparse Core Ops, SparseCore 0:
  55.0 268.8 all-gather.1
where the time goes:
time: 1130 us; the launch traced here: 1110 us
  matrix products  473 us (42%)
  blocking collectives  254 us (22%)
  local copies, waits for them, and re-layouts  234 us (21%)
  waiting for transfers between devices  94.7 us (8%)
  other arithmetic  36.1 us (3%)
  between operations  14 us (1%)
    all_to_all x1, blocking collectives, shards(): lax.all_to_all(returned, 'row', split_axis=0, concat_axis=1, tiled=True)  243 us
    dot_general x12, matrix products, column(): jnp.einsum('hik,khc->ihc', weights, value_col, preferred_element_type=jnp...  231 us
    sub x12, matrix products, column(): weights = jax.nn.softmax(scores, axis=-1).astype(jnp.bfloat16)  202 us
    all_to_all x1, waiting for transfers between devices, shards(): lax.all_to_all(normed, 'row', split_axis=1, concat_axis=0, tiled=True)  94.7 us
    while x4, local copies, waits for them, and re-layouts, shards(): updates = lax.map(column, (query_cols, key_cols, value_cols, gate_cols))  83.8 us
    reshape x3, local copies, waits for them, and re-layouts, heads_first(): values_bf16.reshape(all_rows, own_cols, head_count, head_width)  73.2 us
    dynamic_slice x24, local copies, waits for them, and re-layouts, shards(): updates = lax.map(column, (query_cols, key_cols, value_cols, gate_cols))  43.8 us
    dot_general x4, matrix products, project(): return jnp.dot(flattened, weight, preferred_element_type=jnp.float32)  26.3 us
  transfers between devices with their start and end apart: 2, of which 1 were waited for; matrix products, arithmetic and copies ran while one was open for 18% of the time, Pallas kernels for 0%

commit v1 on v0

v1 whole, which is shorter than its diff:
```python
import functools
import math

import jax
import jax.numpy as jnp
from jax import lax
from jax.experimental import pallas as pl
from jax.experimental.pallas import tpu as pltpu
from jax.sharding import PartitionSpec as P

HEADS = 4
WIDTH = 32
GROUPS = 3
KEY_TILE = 256
LOG2E = 1.4426950408889634
F32 = jnp.float32
BF16 = jnp.bfloat16


def dot_nt(a, b):
    return lax.dot_general(a, b, (((1,), (1,)), ((), ())), preferred_element_type=F32)


def dot_tn(a, b):
    return lax.dot_general(a, b, (((0,), (0,)), ((), ())), preferred_element_type=F32)


def normalize_kernel(pair_ref, gain_ref, shift_ref, bias_ref, *out_refs):
    plane_ref, column_refs = out_refs[0], out_refs[1:]
    rows, cols, channels = pair_ref.shape
    owners, group_cols = column_refs[0].shape[:2]
    own_cols = group_cols * len(column_refs)
    gain, shift = gain_ref[...], shift_ref[...]
    for start in range(0, cols, own_cols * 4):
        width = own_cols * 4
        values = pair_ref[:, start : start + width, :].astype(F32)
        centered = values - jnp.mean(values, axis=-1, keepdims=True)
        variance = jnp.mean(centered * centered, axis=-1, keepdims=True)
        normed = centered * lax.rsqrt(variance + 1e-05) * gain + shift
        by_column = jnp.swapaxes(normed, 0, 1).astype(BF16)
        for owner in range(4):
            for group, ref in enumerate(column_refs):
                first = owner * own_cols + group * group_cols
                ref[start // own_cols + owner] = by_column[first : first + group_cols]
    for row in range(rows):
        values = pair_ref[row].astype(F32)
        centered = values - jnp.mean(values, axis=-1, keepdims=True)
        variance = jnp.mean(centered * centered, axis=-1, keepdims=True)
        normed = (centered * lax.rsqrt(variance + 1e-05) * gain + shift).astype(BF16)
        plane_ref[row] = dot_nt(bias_ref[...], normed)


def attend_kernel(
    order_ref, steps_ref, x_ref, planes_ref, valid_ref, wqg_ref, gate_bias_ref, wk_ref, wv_ref, wo_ref,
    out_ref, bias, keys, values, queries, summed, sems,
):
    blocks, _, block, channels = x_ref.shape
    length = blocks * block
    col_blocks = planes_ref.shape[1]
    col_width = planes_ref.shape[-1]
    steps = steps_ref[0]
    key_blocks = (steps * KEY_TILE + block - 1) // block

    def plane_copy(slot, col):
        return pltpu.make_async_copy(
            planes_ref.at[order_ref[slot], col],
            bias.at[:, pl.ds(pl.multiple_of(slot * block, block), block), pl.ds(col * col_width, col_width)],
            sems.at[0],
        )

    first = pl.program_id(0) == 0

    @pl.when(first)
    def _():
        @pl.loop(0, key_blocks)
        def _(slot):
            for col in range(col_blocks):
                plane_copy(slot, col).start()

    x = x_ref[...].reshape(length, channels)
    projected = dot_nt(wqg_ref[...], x)
    queries[...] = (projected[:channels] * (1.0 / math.sqrt(WIDTH))).astype(BF16)
    gate = jax.nn.sigmoid(projected[channels:] + gate_bias_ref[...])
    compact = jnp.concatenate([x_ref[order_ref[slot], 0] for slot in range(blocks)], axis=0)
    key_all = jnp.dot(compact, wk_ref[...], preferred_element_type=F32).astype(BF16)
    valid = valid_ref[...]
    value_all = (dot_nt(wv_ref[...], compact).astype(BF16).astype(F32) * valid[:1]).astype(BF16)
    ones = jnp.broadcast_to(valid[:1], (16, length)).astype(BF16)
    for head in range(HEADS):
        lanes = slice(head * WIDTH, (head + 1) * WIDTH)
        keys[head] = key_all[:, lanes]
        values[head, :WIDTH] = value_all[lanes]
        values[head, WIDTH:] = ones

    @pl.when(first)
    def _():
        @pl.loop(0, key_blocks)
        def _(slot):
            for col in range(col_blocks):
                plane_copy(slot, col).wait()

    def scores(head, at):
        heads = pl.ds(head * WIDTH, WIDTH)
        raw = jnp.dot(keys[head, at, :], queries[heads, :], preferred_element_type=F32)
        return raw + bias[head, at, :].astype(F32)

    def tile(step):
        return pl.ds(pl.multiple_of(step * KEY_TILE, KEY_TILE), KEY_TILE)

    summed[...] = jnp.zeros_like(summed)

    @pl.loop(0, steps)
    def _(step):
        at = tile(step)
        for head in range(HEADS):
            weights = jnp.exp(scores(head, at)).astype(BF16)
            summed[head] += jnp.dot(values[head, :, at], weights, preferred_element_type=F32)

    totals = summed[:, WIDTH, :]
    lowest, highest = jnp.min(totals), jnp.max(totals)
    safe = jnp.logical_and(lowest > 2.0**-60, highest < 2.0**100)

    @pl.when(jnp.logical_not(safe))
    def _():
        for head in range(HEADS):
            def masked(step):
                at = tile(step)
                real = jnp.transpose(valid_ref[:, at])[:, :1] > 0
                return at, jnp.where(real, scores(head, at), -3.0e38)

            def highest_of(step, top):
                return jnp.maximum(top, jnp.max(masked(step)[1], axis=0, keepdims=True))

            top = lax.fori_loop(0, steps, highest_of, jnp.full((1, length), -3.0e38, F32))
            summed[head] = jnp.zeros_like(summed[head])

            @pl.loop(0, steps)
            def _(step):
                at, shifted = masked(step)
                weights = jnp.exp(shifted - top).astype(BF16)
                summed[head] += jnp.dot(values[head, :, at], weights, preferred_element_type=F32)

    attended = jnp.concatenate(
        [summed[head, :WIDTH] / summed[head, WIDTH : WIDTH + 1] for head in range(HEADS)], axis=0
    )
    hidden = (gate * attended).astype(BF16)
    update = dot_tn(hidden, wo_ref[...]).astype(BF16)
    out_ref[...] = update.reshape(out_ref.shape)


def normalize(pair_map, ln_gain, ln_bias, w_bias, owners):
    rows, cols, channels = pair_map.shape
    own_cols = cols // owners
    group_cols = own_cols // GROUPS
    block = 16
    padded = jnp.zeros((8, channels), BF16).at[:HEADS].set(w_bias.T)
    group = jax.ShapeDtypeStruct((owners, group_cols, rows, channels), BF16)
    full = pl.BlockSpec((1, channels), lambda i: (0, 0))
    return pl.pallas_call(
        normalize_kernel,
        grid=(rows // block,),
        in_specs=[
            pl.BlockSpec((block, cols, channels), lambda i: (i, 0, 0)),
            full,
            full,
            pl.BlockSpec((8, channels), lambda i: (0, 0)),
        ],
        out_specs=[pl.BlockSpec((block, 8, cols), lambda i: (i, 0, 0))]
        + [pl.BlockSpec((owners, group_cols, block, channels), lambda i: (0, 0, i, 0))] * GROUPS,
        out_shape=[jax.ShapeDtypeStruct((rows, 8, cols), F32)] + [group] * GROUPS,
        compiler_params=pltpu.CompilerParams(vmem_limit_bytes=56 * 2**20),
        name="normalize",
    )(pair_map, ln_gain[None], ln_bias[None], padded)


def attend(x, planes, order, steps, valid, wqg, gate_bias, wk, wv, wo):
    blocks, cols, block, channels = x.shape
    length = blocks * block
    whole = lambda shape: pl.BlockSpec(shape, lambda j, *_: (0,) * len(shape))
    column = pl.BlockSpec((blocks, 1, block, channels), lambda j, *_: (0, j, 0, 0))
    scores = cols * HEADS * length * length
    return pl.pallas_call(
        attend_kernel,
        grid_spec=pltpu.PrefetchScalarGridSpec(
            num_scalar_prefetch=2,
            grid=(cols,),
            in_specs=[
                column,
                pl.BlockSpec(memory_space=pl.ANY),
                whole(valid.shape),
                whole(wqg.shape),
                whole(gate_bias.shape),
                whole(wk.shape),
                whole(wv.shape),
                whole(wo.shape),
            ],
            out_specs=column,
            scratch_shapes=[
                pltpu.VMEM((HEADS, length, length), BF16),
                pltpu.VMEM((HEADS, length, WIDTH), BF16),
                pltpu.VMEM((HEADS, WIDTH + 16, length), BF16),
                pltpu.VMEM((channels, length), BF16),
                pltpu.VMEM((HEADS, WIDTH + 16, length), F32),
                pltpu.SemaphoreType.DMA((1,)),
            ],
        ),
        out_shape=jax.ShapeDtypeStruct(x.shape, BF16),
        compiler_params=pltpu.CompilerParams(vmem_limit_bytes=60 * 2**20),
        cost_estimate=pl.CostEstimate(
            flops=scores * 512, bytes_accessed=planes.size * 2 + x.size * 4, transcendentals=scores
        ),
        name="attend",
    )(order, steps, x, planes, valid, wqg, gate_bias, wk, wv, wo)


def shards(
    pair_map, valid_tokens, ln_gain, ln_bias, w_bias, w_query, w_key, w_value, w_gate, gate_bias, w_out,
):
    rows, cols, channels = pair_map.shape
    owners = lax.axis_size("row")
    length = valid_tokens.shape[0]
    planes, *groups = normalize(pair_map, ln_gain, ln_bias, w_bias, owners)
    planes = jnp.swapaxes(planes[:, :HEADS], 0, 1).astype(BF16)
    received = [lax.all_to_all(group, "row", split_axis=0, concat_axis=0) for group in groups]
    planes = lax.all_gather(planes, "col")
    planes = lax.all_gather(planes, "row")

    blocks = valid_tokens.reshape(owners, rows)
    empty = jnp.max(blocks, axis=1) == 0
    order = jnp.argsort(empty, stable=True).astype(jnp.int32)
    filled = jnp.sum(jnp.logical_not(empty).astype(jnp.int32))
    steps = ((filled * rows + KEY_TILE - 1) // KEY_TILE).reshape(1).astype(jnp.int32)
    valid = jnp.broadcast_to(blocks[order].reshape(1, length).astype(F32), (8, length))
    wqg = jnp.concatenate([w_query, w_gate], axis=1).T
    arguments = (planes, order, steps, valid, wqg, gate_bias[:, None], w_key, w_value.T, w_out)
    returned = []
    for group in received:
        update = attend(group, *arguments)
        returned.append(lax.all_to_all(update, "row", split_axis=0, concat_axis=0))
    update = jnp.concatenate(returned, axis=1).reshape(cols, rows, channels)
    return jnp.swapaxes(update, 0, 1)


def solution(mesh):
    return jax.shard_map(
        shards,
        mesh=mesh,
        in_specs=(P("row", "col", None), P(), P(), P(), P(), P(), P(), P(), P(), P(), P()),
        out_specs=P("row", "col", None),
        check_vma=False,
    )
```

time: 1130 us -> 784 us (0.69); the launches traced: 1110 us -> 783 us
  matrix products: 473 us -> 0 us
  Pallas kernels: 0 us -> 449 us
  local copies, waits for them, and re-layouts: 234 us -> 11.2 us
  starting transfers between devices: 8.07 us -> 207 us
  blocking collectives: 254 us -> 83.6 us
  waiting for transfers between devices: 94.7 us -> 14.5 us
  other arithmetic: 36.1 us -> 3.52 us
    pallas_call x0 -> x4, Pallas kernels: none -> 449 us  [the longest x3 433 us: attend(): pl.pallas_call(attend_kernel, grid_spec=pltpu.PrefetchScalarGridSpec(num_...]
    dot_general x29 -> x0, matrix products: 271 us -> none  [the longest x12 231 us: column(): jnp.einsum('hik,khc->ihc', weights, value_col, preferred_element_type=jnp...]
    sub x12 -> x0, matrix products: 202 us -> none  [column(): weights = jax.nn.softmax(scores, axis=-1).astype(jnp.bfloat16)]
    all_to_all x1 -> x4, starting transfers between devices: 8.07 us -> 207 us  [the longest x2 190 us: shards(): lax.all_to_all(group, 'row', split_axis=0, concat_axis=0)]
    all_to_all x1 -> x2, blocking collectives: 243 us -> 73.2 us  [the longest x1 46.5 us: shards(): lax.all_to_all(group, 'row', split_axis=0, concat_axis=0)]
    reshape x5 -> x2, local copies, waits for them, and re-layouts: 93.5 us -> 3.48 us  [the longest x1 3.4 us: shards(): update = jnp.concatenate(returned, axis=1).reshape(cols, rows, channels)]
    while x4 -> x0, local copies, waits for them, and re-layouts: 83.8 us -> none  [shards(): updates = lax.map(column, (query_cols, key_cols, value_cols, gate_cols))]
    all_to_all x1 -> x4, waiting for transfers between devices: 94.7 us -> 14.5 us  [the longest x2 14.5 us: shards(): lax.all_to_all(group, 'row', split_axis=0, concat_axis=0)]
  transfers between devices with their start and end apart: 2 -> 5, of which waited for: 1 -> 1; matrix products, arithmetic and copies ran while one was open for 18% -> 1% of each run, Pallas kernels for 0% -> 55%
where the time goes in v1:
time: 784 us; the launch traced here: 783 us
  Pallas kernels  449 us (57%)
  starting transfers between devices  207 us (26%)
  blocking collectives  83.6 us (11%)
  waiting for transfers between devices  14.5 us (2%)
  between operations  14.3 us (2%)
  local copies, waits for them, and re-layouts  11.2 us (1%)
    pallas_call x3, Pallas kernels, attend(): pl.pallas_call(attend_kernel, grid_spec=pltpu.PrefetchScalarGridSpec(num_...  433 us
    all_to_all x2, starting transfers between devices, shards(): lax.all_to_all(group, 'row', split_axis=0, concat_axis=0)  190 us
    all_to_all x1, blocking collectives, shards(): lax.all_to_all(group, 'row', split_axis=0, concat_axis=0)  46.5 us
    all_to_all x1, blocking collectives, shards(): returned.append(lax.all_to_all(update, 'row', split_axis=0, concat_axis=0))  26.6 us
    all_to_all x2, starting transfers between devices, shards(): returned.append(lax.all_to_all(update, 'row', split_axis=0, concat_axis=0))  16.7 us
  transfers between devices with their start and end apart: 5, of which 1 were waited for; matrix products, arithmetic and copies ran while one was open for 1% of the time, Pallas kernels for 55%

profile of v1, /device:TPU:0, one launch (start us, length us, event | category | flops | bytes accessed | tf_op | source)
XLA Modules:
  0.0 782.8 jit_solution(15010816228972050517)
XLA Ops:
  6.5 1.3 scatter.4.bias_ref
  7.8 15.6 %normalize.1 = (f32[48,8,384]{2,1,0:T(8,128)}, bf16[32,4,48,128]{3,2,1,0:T(8,128)(2,1)}, bf16[32,4,48,128]{3,2,1,0:T(8,128)(2,1)}, bf16[32,4,48,128]{3,2,1,0:T(8,128)(2,1)}) custom-call(bf16[48,384,128]{2,1,0:T(8,128)(2,1)} %pair_ref.1, f32[1,128]{1,0:T(1,128)} %bitcast.22, f32[1,128]{1,0:T(1,128)} %bitcast.23, bf16[8,128]{1,0:T(8,128)(2,1)} %scatter.4.bias_ref), custom_call_target="tpu_custom_call" | custom-call | tf_op jit(solution)/shard_map/normalize/pallas_call | solution.py:159
  23.4 1.2 fusion
  24.7 10.4 %all-gather = bf16[16,48,384]{2,1,0:T(8,128)(2,1)} all-gather(bf16[4,48,384]{2,1,0:T(8,128)(2,1)S(1)} %copy.20), channel_id=2, replica_groups=mesh['row'=32,'col'=4] {'col'}, dimensions={0}, use_global_device_ids=true | all-gather | bytes 737280 | tf_op jit(solution)/shard_map/all_gather | solution.py:225
  35.1 46.5 %all_to_all.30.x_ref = bf16[32,4,48,128]{3,2,1,0:T(8,128)(2,1)} all-to-all(bf16[32,4,48,128]{3,2,1,0:T(8,128)(2,1)S(1)} %copy-done.2), channel_id=1, replica_groups=mesh['row'=32,'col'=4] {'row'}, dimensions={0} | all-to-all | bytes 3145728 | tf_op jit(solution)/shard_map/all_to_all | solution.py:224
  81.7 185.2 %all-to-all-start.2 = ((bf16[32,4,48,128]{3,2,1,0:T(8,128)(2,1)}), bf16[32,4,48,128]{3,2,1,0:T(8,128)(2,1)S(1)}, u32[]{:S(2)}, u32[]{:S(2)}) async-start(bf16[32,4,48,128]{3,2,1,0:T(8,128)(2,1)} %get-tuple-element.25), calls=%async_computation.2 | async-start | bytes 3145728 | tf_op jit(solution)/shard_map/all_to_all | solution.py:224
  267.1 0.6 fusion.1
  268.4 1.6 sort.17
  270.0 0.6 gather_fusion
  270.8 0.7 copy.23
  271.7 0.7 copy.24.gate_bias_ref
  272.4 0.6 maximum_bitcast_fusion.wqg_ref
  273.0 14.4 %all-to-all-done.2.x_ref = bf16[32,4,48,128]{3,2,1,0:T(8,128)(2,1)S(1)} async-done(((bf16[32,4,48,128]{3,2,1,0:T(8,128)(2,1)}), bf16[32,4,48,128]{3,2,1,0:T(8,128)(2,1)S(1)}, u32[]{:S(2)}, u32[]{:S(2)}) %all-to-all-start.2) | async-done | bytes 1572896 | tf_op jit(solution)/shard_map/all_to_all | solution.py:224
  287.5 1.1 copy-done
  288.6 5.1 all-to-all-start.4
  293.8 0.6 broadcast_in_dim.21.valid_ref
  294.4 144.4 %attend.3 = bf16[32,4,48,128]{3,2,1,0:T(8,128)(2,1)} custom-call(s32[32]{0:T(128)} %copy-done.8, s32[1]{0:T(128)} %bitcast.steps_ref, bf16[32,4,48,128]{3,2,1,0:T(8,128)(2,1)} %all_to_all.30.x_ref, bf16[32,4,4,48,384]{4,3,2,1,0:T(8,128)(2,1)} %bitcast.25, f32[8,1536]{1,0:T(8,128)} %broadcast_in_dim.21.valid_ref, ...), custom_call_target="tpu_custom_call" | custom-call | flops 19327352832 | bytes 22020096 | tf_op jit(solution)/shard_map/attend/pallas_call | solution.py:182
  438.8 1.1 copy-done.1
  440.0 8.3 %all-to-all-start.1 = ((bf16[32,4,48,128]{3,2,1,0:T(8,128)(2,1)}), bf16[32,4,48,128]{3,2,1,0:T(8,128)(2,1)S(1)}, u32[]{:S(2)}, u32[]{:S(2)}) async-start(bf16[32,4,48,128]{3,2,1,0:T(8,128)(2,1)} %attend.3), calls=%async_computation.1 | async-start | bytes 3145728 | tf_op jit(solution)/shard_map/all_to_all | solution.py:239
  448.3 144.4 %attend.4 = bf16[32,4,48,128]{3,2,1,0:T(8,128)(2,1)} custom-call(s32[32]{0:T(128)} %copy-done.8, s32[1]{0:T(128)} %bitcast.steps_ref, bf16[32,4,48,128]{3,2,1,0:T(8,128)(2,1)} %copy-done, bf16[32,4,4,48,384]{4,3,2,1,0:T(8,128)(2,1)} %bitcast.26, f32[8,1536]{1,0:T(8,128)} %broadcast_in_dim.21.valid_ref, bf16[256,128]{1,0:T(8,128)(2,1)} %maximum_bitcast_fusion.wqg_ref, ...), custom_call_target="tpu_custom_call" | custom-call | flops 19327352832 | bytes 22020096 | tf_op jit(solution)/shard_map/attend/pallas_call | solution.py:182
  592.7 8.4 %all-to-all-start.3 = ((bf16[32,4,48,128]{3,2,1,0:T(8,128)(2,1)}), bf16[32,4,48,128]{3,2,1,0:T(8,128)(2,1)S(1)}, u32[]{:S(2)}, u32[]{:S(2)}) async-start(bf16[32,4,48,128]{3,2,1,0:T(8,128)(2,1)} %attend.4), calls=%async_computation.3 | async-start | bytes 3145728 | tf_op jit(solution)/shard_map/all_to_all | solution.py:239
  601.0 144.4 %attend.5 = bf16[32,4,48,128]{3,2,1,0:T(8,128)(2,1)} custom-call(s32[32]{0:T(128)} %copy-done.8, s32[1]{0:T(128)} %bitcast.steps_ref, bf16[32,4,48,128]{3,2,1,0:T(8,128)(2,1)} %copy-done.1, bf16[32,4,4,48,384]{4,3,2,1,0:T(8,128)(2,1)} %bitcast.27, f32[8,1536]{1,0:T(8,128)} %broadcast_in_dim.21.valid_ref, bf16[256,128]{1,0:T(8,128)(2,1)} %maximum_bitcast_fusion.wqg_ref, ...), custom_call_target="tpu_custom_call" | custom-call | flops 19327352832 | bytes 22020096 | tf_op jit(solution)/shard_map/attend/pallas_call | solution.py:182
  745.4 26.6 %all_to_all.31 = bf16[32,4,48,128]{3,2,1,0:T(8,128)(2,1)S(1)} all-to-all(bf16[32,4,48,128]{3,2,1,0:T(8,128)(2,1)} %attend.5), channel_id=1, replica_groups=mesh['row'=32,'col'=4] {'row'}, dimensions={0} | all-to-all | bytes 3145728 | tf_op jit(solution)/shard_map/all_to_all | solution.py:239
  772.6 3.4 copy.29
  (34 shorter events, 1.1 us)
Async XLA Ops:
  6.5 287.2 %all-gather.4.cloned.1.call-start = ((), (), s32[]{:S(2)}) async-start(), calls=%async_computation.6 | async-start | bytes 19464192 | tf_op jit(solution)/shard_map/all_gather | solution.py:226
  23.4 11.7 %copy-start.2 = (bf16[32,4,48,128]{3,2,1,0:T(8,128)(2,1)S(1)}, bf16[32,4,48,128]{3,2,1,0:T(8,128)(2,1)}, u32[]{:S(2)}) copy-start(bf16[32,4,48,128]{3,2,1,0:T(8,128)(2,1)} %get-tuple-element.23) | copy-start | bytes 4718596
  81.7 185.2 %copy-start.6 = (s32[1536]{0:T(1024)S(1)}, s32[1536]{0:T(1024)}, u32[]{:S(2)}) copy-start(s32[1536]{0:T(1024)} %param.14) | copy-start | bytes 18436
  81.7 189.0 %copy-start.3 = (bf16[128,128]{1,0:T(8,128)(2,1)S(1)}, bf16[128,128]{1,0:T(8,128)(2,1)}, u32[]{:S(2)}) copy-start(bf16[128,128]{1,0:T(8,128)(2,1)} %param.18) | copy-start | bytes 98308
  81.7 189.1 %copy-start.4 = (bf16[128,128]{1,0:T(8,128)(2,1)S(1)}, bf16[128,128]{1,0:T(8,128)(2,1)}, u32[]{:S(2)}) copy-start(bf16[128,128]{1,0:T(8,128)(2,1)} %param.20) | copy-start | bytes 98308
  81.7 189.8 %copy-start.5 = (bf16[128,128]{1,0:T(8,128)(2,1)S(1)}, bf16[128,128]{1,0:T(8,128)(2,1)}, u32[]{:S(2)}) copy-start(bf16[128,128]{1,0:T(8,128)(2,1)} %param.21) | copy-start | bytes 98308
  81.7 190.0 %copy-start.7 = (f32[128]{0:T(128)S(1)}, f32[128]{0:T(128)}, u32[]{:S(2)}) copy-start(f32[128]{0:T(128)} %param.22) | copy-start | bytes 1540
  81.7 205.8 %all-to-all-start.2 = ((bf16[32,4,48,128]{3,2,1,0:T(8,128)(2,1)}), bf16[32,4,48,128]{3,2,1,0:T(8,128)(2,1)S(1)}, u32[]{:S(2)}, u32[]{:S(2)}) async-start(bf16[32,4,48,128]{3,2,1,0:T(8,128)(2,1)} %get-tuple-element.25), calls=%async_computation.2 | async-start | bytes 3145728 | tf_op jit(solution)/shard_map/all_to_all | solution.py:224
  270.0 17.5 %copy-start.8 = (s32[32]{0:T(128)}, s32[32]{0:T(128)S(1)}, u32[]{:S(2)}) copy-start(s32[32]{0:T(128)S(1)} %get-tuple-element.22.order_ref) | copy-start | bytes 388
  287.5 1.1 copy-start
  288.6 150.2 %all-to-all-start.4 = ((bf16[32,4,48,128]{3,2,1,0:T(8,128)(2,1)}), bf16[32,4,48,128]{3,2,1,0:T(8,128)(2,1)S(1)}, u32[]{:S(2)}, u32[]{:S(2)}) async-start(bf16[32,4,48,128]{3,2,1,0:T(8,128)(2,1)} %get-tuple-element.26), calls=%async_computation.4 | async-start | bytes 3145728 | tf_op jit(solution)/shard_map/all_to_all | solution.py:224
  438.8 1.1 copy-start.1
  440.0 152.7 %all-to-all-start.1 = ((bf16[32,4,48,128]{3,2,1,0:T(8,128)(2,1)}), bf16[32,4,48,128]{3,2,1,0:T(8,128)(2,1)S(1)}, u32[]{:S(2)}, u32[]{:S(2)}) async-start(bf16[32,4,48,128]{3,2,1,0:T(8,128)(2,1)} %attend.3), calls=%async_computation.1 | async-start | bytes 3145728 | tf_op jit(solution)/shard_map/all_to_all | solution.py:239
  592.7 152.7 %all-to-all-start.3 = ((bf16[32,4,48,128]{3,2,1,0:T(8,128)(2,1)}), bf16[32,4,48,128]{3,2,1,0:T(8,128)(2,1)S(1)}, u32[]{:S(2)}, u32[]{:S(2)}) async-start(bf16[32,4,48,128]{3,2,1,0:T(8,128)(2,1)} %attend.4), calls=%async_computation.3 | async-start | bytes 3145728 | tf_op jit(solution)/shard_map/all_to_all | solution.py:239
Sparse Core Ops, SparseCore 0:
  35.3 228.8 all-gather.3

commit v2 on v1

--- a/solution.py
+++ b/solution.py
@@ -56,14 +56,15 @@
 ):
     blocks, _, block, channels = x_ref.shape
     length = blocks * block
-    col_blocks = planes_ref.shape[1]
+    col_blocks = 4
     col_width = planes_ref.shape[-1]
     steps = steps_ref[0]
     key_blocks = (steps * KEY_TILE + block - 1) // block
 
     def plane_copy(slot, col):
+        row = order_ref[slot]
         return pltpu.make_async_copy(
-            planes_ref.at[order_ref[slot], col],
+            planes_ref.at[col % 2, row % 4, row // 8, col // 2 * 2 + row // 4 % 2],
             bias.at[:, pl.ds(pl.multiple_of(slot * block, block), block), pl.ds(col * col_width, col_width)],
             sems.at[0],
         )
@@ -146,6 +147,115 @@
     hidden = (gate * attended).astype(BF16)
     update = dot_tn(hidden, wo_ref[...]).astype(BF16)
     out_ref[...] = update.reshape(out_ref.shape)
+
+
+def gather_kernel(own_ref, all_ref, own_sem, send_sems, recv_sems, pair_send, pair_recv):
+    row, col = lax.axis_index("row"), lax.axis_index("col")
+    core = col % 2
+    here = {"x": row % 4, "y": row // 8, "z": col // 2 * 2 + row // 4 % 2}
+
+    def device(place, on_core):
+        return ((place["y"] * 2 + place["z"] % 2) * 4 + place["x"], place["z"] // 2 * 2 + on_core)
+
+    def moved(axis, by):
+        return {**here, axis: (here[axis] + by) % 4}
+
+    partner = device(here, 1 - core)
+    barrier = pltpu.get_barrier_semaphore()
+    friends = [device(moved(axis, by), core) for axis in "xyz" for by in (1, 3)] + [partner]
+    for friend in friends:
+        pl.semaphore_signal(barrier, inc=1, device_id=friend, device_id_type=pl.DeviceIdType.MESH)
+    pl.semaphore_wait(barrier, len(friends))
+
+    mine = pltpu.make_async_copy(own_ref, all_ref.at[core, here["x"], here["y"], here["z"]], own_sem)
+    mine.start()
+    mine.wait()
+    orders = ("zyx", "xzy", "yxz")
+
+    def region(part, stage, by, heads):
+        place = []
+        for axis in "xyz":
+            at = orders[part].index(axis)
+            if at < stage:
+                place.append(slice(None))
+            elif at == stage:
+                place.append((here[axis] + by) % 4)
+            else:
+                place.append(here[axis])
+        return all_ref.at[(core, *place, heads, pl.ds(part * 16, 16))]
+
+    every, low, high = slice(None), pl.ds(0, 2), pl.ds(2, 2)
+
+    def send(part, stage, kind, by, heads, to):
+        ref = region(part, stage, by, heads)
+        copy = pltpu.make_async_remote_copy(
+            src_ref=ref,
+            dst_ref=ref,
+            send_sem=send_sems.at[part, stage, kind],
+            recv_sem=recv_sems.at[part, stage, kind],
+            device_id=device(moved(orders[part][stage], to), core),
+            device_id_type=pl.DeviceIdType.MESH,
+        )
+        copy.start()
+        return copy
+
+    def pair(part, piece, by):
+        ref = region(part, 2, by, every)
+        copy = pltpu.make_async_remote_copy(
+            src_ref=ref,
+            dst_ref=ref,
+            send_sem=pair_send.at[part, piece],
+            recv_sem=pair_recv.at[part, piece],
+            device_id=partner,
+            device_id_type=pl.DeviceIdType.MESH,
+        )
+        copy.start()
+        return copy
+
+    copies, pairs = [], []
+    for stage in range(3):
+        last = stage == 2
+        near = []
+        for part in range(3):
+            near.append((send(part, stage, 0, 0, every, 1), send(part, stage, 1, 0, every, 3)))
+            if last:
+                pairs.append(pair(part, 0, 0))
+        far = []
+        for part in range(3):
+            near[part][0].wait_recv()
+            near[part][1].wait_recv()
+            far.append((send(part, stage, 2, 3, low, 1), send(part, stage, 3, 1, high, 3)))
+            if last:
+                pairs += [pair(part, 1, 3), pair(part, 2, 1)]
+        for part in range(3):
+            far[part][0].wait_recv()
+            far[part][1].wait_recv()
+            if last:
+                pairs.append(pair(part, 3, 2))
+        copies += [copy for two in near + far for copy in two]
+    for copy in copies:
+        copy.wait_send()
+    for copy in pairs:
+        copy.wait()
+
+
+def gather(planes):
+    heads, rows, cols = planes.shape
+    return pl.pallas_call(
+        gather_kernel,
+        in_specs=[pl.BlockSpec(memory_space=pl.ANY)],
+        out_specs=pl.BlockSpec(memory_space=pl.ANY),
+        out_shape=jax.ShapeDtypeStruct((2, 4, 4, 4, heads, rows, cols), BF16),
+        scratch_shapes=[
+            pltpu.SemaphoreType.DMA,
+            pltpu.SemaphoreType.DMA((3, 3, 4)),
+            pltpu.SemaphoreType.DMA((3, 3, 4)),
+            pltpu.SemaphoreType.DMA((3, 4)),
+            pltpu.SemaphoreType.DMA((3, 4)),
+        ],
+        compiler_params=pltpu.CompilerParams(collective_id=0, has_side_effects=True),
+        name="gather_planes",
+    )(planes)
 
 
 def normalize(pair_map, ln_gain, ln_bias, w_bias, owners):
@@ -222,8 +332,7 @@
     planes, *groups = normalize(pair_map, ln_gain, ln_bias, w_bias, owners)
     planes = jnp.swapaxes(planes[:, :HEADS], 0, 1).astype(BF16)
     received = [lax.all_to_all(group, "row", split_axis=0, concat_axis=0) for group in groups]
-    planes = lax.all_gather(planes, "col")
-    planes = lax.all_gather(planes, "row")
+    planes = gather(planes)
 
     blocks = valid_tokens.reshape(owners, rows)
     empty = jnp.max(blocks, axis=1) == 0

time: 784 us -> 696 us (0.89)
  starting transfers between devices: 207 us -> 26.2 us
  Pallas kernels: 449 us -> 592 us
  blocking collectives: 83.6 us -> 61.4 us
  waiting for transfers between devices: 14.5 us -> 0.01 us
  between operations: 14.3 us -> 0.89 us
    all_to_all x2, starting transfers between devices: 190 us -> 9.53 us  [shards(): lax.all_to_all(group, 'row', split_axis=0, concat_axis=0)]
    pallas_call x3, Pallas kernels: 433 us -> 514 us  [attend(): pl.pallas_call(attend_kernel, grid_spec=pltpu.PrefetchScalarGridSpec(num_...]
    pallas_call x0 -> x1, Pallas kernels: none -> 62.8 us  [gather(): pl.pallas_call(gather_kernel, in_specs=[pl.BlockSpec(memory_space=pl.ANY)...]
    all_to_all x1, blocking collectives: 46.5 us -> 31.7 us  [shards(): lax.all_to_all(group, 'row', split_axis=0, concat_axis=0)]
    all_to_all x2, waiting for transfers between devices: 14.5 us -> 0.01 us  [shards(): lax.all_to_all(group, 'row', split_axis=0, concat_axis=0)]
    all_gather x1 -> x0, blocking collectives: 10.4 us -> none  [shards(): planes = lax.all_gather(planes, 'col')]
  transfers between devices with their start and end apart: 5 -> 4, of which waited for: 1 -> 0; matrix products, arithmetic and copies ran while one was open for 1% -> 1% of each run, Pallas kernels for 55% -> 83%
where the time goes in v2:
time: 696 us; the launch traced here: 695 us
  Pallas kernels  592 us (85%)
  blocking collectives  61.4 us (9%)
  starting transfers between devices  26.2 us (4%)
  local copies, waits for them, and re-layouts  10.8 us (2%)
    pallas_call x3, Pallas kernels, attend(): pl.pallas_call(attend_kernel, grid_spec=pltpu.PrefetchScalarGridSpec(num_...  514 us
    pallas_call x1, Pallas kernels, gather(): pl.pallas_call(gather_kernel, in_specs=[pl.BlockSpec(memory_space=pl.ANY)...  62.8 us
    all_to_all x1, blocking collectives, shards(): lax.all_to_all(group, 'row', split_axis=0, concat_axis=0)  31.7 us
    all_to_all x1, blocking collectives, shards(): returned.append(lax.all_to_all(update, 'row', split_axis=0, concat_axis=0))  29.7 us
    all_to_all x2, starting transfers between devices, shards(): returned.append(lax.all_to_all(update, 'row', split_axis=0, concat_axis=0))  16.7 us
    pallas_call x1, Pallas kernels, normalize(): pl.pallas_call(normalize_kernel, grid=(rows // block,), in_specs=[pl.Bloc...  15.6 us
  transfers between devices with their start and end apart: 4, of which 0 were waited for; matrix products, arithmetic and copies ran while one was open for 1% of the time, Pallas kernels for 83%

profile of v2, /device:TPU:0, one launch (start us, length us, event | category | flops | bytes accessed | tf_op | source)
XLA Modules:
  0.0 695.3 jit_solution(15505995061045388724)
XLA Ops:
  0.0 1.3 scatter.4.bias_ref
  1.3 15.6 %normalize.1 = (f32[48,8,384]{2,1,0:T(8,128)}, bf16[32,4,48,128]{3,2,1,0:T(8,128)(2,1)}, bf16[32,4,48,128]{3,2,1,0:T(8,128)(2,1)}, bf16[32,4,48,128]{3,2,1,0:T(8,128)(2,1)}) custom-call(bf16[48,384,128]{2,1,0:T(8,128)(2,1)} %pair_ref.1, f32[1,128]{1,0:T(1,128)} %bitcast.19, f32[1,128]{1,0:T(1,128)} %bitcast.20, bf16[8,128]{1,0:T(8,128)(2,1)} %scatter.4.bias_ref), custom_call_target="tpu_custom_call" | custom-call | tf_op jit(solution)/shard_map/normalize/pallas_call | solution.py:269
  16.9 31.7 %all_to_all.30.x_ref = bf16[32,4,48,128]{3,2,1,0:T(8,128)(2,1)} all-to-all(bf16[32,4,48,128]{3,2,1,0:T(8,128)(2,1)} %get-tuple-element.23), channel_id=1, replica_groups=mesh['row'=32,'col'=4] {'row'}, dimensions={0} | all-to-all | bytes 3145728 | tf_op jit(solution)/shard_map/all_to_all | solution.py:334
  48.6 4.3 all-to-all-start.2
  53.2 0.6 fusion.1
  54.5 1.6 sort.17
  56.1 0.6 gather_fusion
  56.9 0.7 copy.15
  57.7 0.7 copy.16.gate_bias_ref
  58.6 0.7 fusion.own_ref
  59.3 62.8 %gather_planes.1.planes_ref = bf16[2,4,4,4,4,48,384]{6,5,4,3,2,1,0:T(8,128)(2,1)} custom-call(bf16[4,48,384]{2,1,0:T(8,128)(2,1)} %fusion.own_ref), custom_call_target="tpu_custom_call" | custom-call | tf_op jit(solution)/shard_map/gather_planes/pallas_call | solution.py:244
  122.1 0.6 maximum_bitcast_fusion.wqg_ref
  122.8 1.2 copy-done
  124.0 5.2 all-to-all-start.4
  129.2 0.6 broadcast_in_dim.21.valid_ref
  129.8 171.3 %attend.3 = bf16[32,4,48,128]{3,2,1,0:T(8,128)(2,1)} custom-call(s32[32]{0:T(128)} %copy-done.8, s32[1]{0:T(128)} %bitcast.steps_ref, bf16[32,4,48,128]{3,2,1,0:T(8,128)(2,1)} %all_to_all.30.x_ref, bf16[2,4,4,4,4,48,384]{6,5,4,3,2,1,0:T(8,128)(2,1)} %gather_planes.1.planes_ref, f32[8,1536]{1,0:T(8,128)} %broadcast_in_dim.21.valid_ref, ...), custom_call_target="tpu_custom_call" | custom-call | flops 19327352832 | bytes 22020096 | tf_op jit(solution)/shard_map/attend/pallas_call | solution.py:292
  301.2 1.1 copy-done.1
  302.3 8.3 %all-to-all-start.1 = ((bf16[32,4,48,128]{3,2,1,0:T(8,128)(2,1)}), bf16[32,4,48,128]{3,2,1,0:T(8,128)(2,1)S(1)}, u32[]{:S(2)}, u32[]{:S(2)}) async-start(bf16[32,4,48,128]{3,2,1,0:T(8,128)(2,1)} %attend.3), calls=%async_computation.1 | async-start | bytes 3145728 | tf_op jit(solution)/shard_map/all_to_all | solution.py:348
  310.6 171.3 %attend.4 = bf16[32,4,48,128]{3,2,1,0:T(8,128)(2,1)} custom-call(s32[32]{0:T(128)} %copy-done.8, s32[1]{0:T(128)} %bitcast.steps_ref, bf16[32,4,48,128]{3,2,1,0:T(8,128)(2,1)} %copy-done, bf16[2,4,4,4,4,48,384]{6,5,4,3,2,1,0:T(8,128)(2,1)} %gather_planes.1.planes_ref, f32[8,1536]{1,0:T(8,128)} %broadcast_in_dim.21.valid_ref, ...), custom_call_target="tpu_custom_call" | custom-call | flops 19327352832 | bytes 22020096 | tf_op jit(solution)/shard_map/attend/pallas_call | solution.py:292
  482.0 8.4 %all-to-all-start.3 = ((bf16[32,4,48,128]{3,2,1,0:T(8,128)(2,1)}), bf16[32,4,48,128]{3,2,1,0:T(8,128)(2,1)S(1)}, u32[]{:S(2)}, u32[]{:S(2)}) async-start(bf16[32,4,48,128]{3,2,1,0:T(8,128)(2,1)} %attend.4), calls=%async_computation.3 | async-start | bytes 3145728 | tf_op jit(solution)/shard_map/all_to_all | solution.py:348
  490.3 171.3 %attend.5 = bf16[32,4,48,128]{3,2,1,0:T(8,128)(2,1)} custom-call(s32[32]{0:T(128)} %copy-done.8, s32[1]{0:T(128)} %bitcast.steps_ref, bf16[32,4,48,128]{3,2,1,0:T(8,128)(2,1)} %copy-done.1, bf16[2,4,4,4,4,48,384]{6,5,4,3,2,1,0:T(8,128)(2,1)} %gather_planes.1.planes_ref, f32[8,1536]{1,0:T(8,128)} %broadcast_in_dim.21.valid_ref, ...), custom_call_target="tpu_custom_call" | custom-call | flops 19327352832 | bytes 22020096 | tf_op jit(solution)/shard_map/attend/pallas_call | solution.py:292
  661.7 29.7 %all_to_all.31 = bf16[32,4,48,128]{3,2,1,0:T(8,128)(2,1)S(1)} all-to-all(bf16[32,4,48,128]{3,2,1,0:T(8,128)(2,1)} %attend.5), channel_id=1, replica_groups=mesh['row'=32,'col'=4] {'row'}, dimensions={0} | all-to-all | bytes 3145728 | tf_op jit(solution)/shard_map/all_to_all | solution.py:348
  691.4 0.5 pad_maximum_fusion
  691.9 3.4 copy.21
  (31 shorter events, 0.7 us)
Async XLA Ops:
  48.6 4.4 copy-start.6
  48.6 8.2 %copy-start.3 = (bf16[128,128]{1,0:T(8,128)(2,1)S(1)}, bf16[128,128]{1,0:T(8,128)(2,1)}, u32[]{:S(2)}) copy-start(bf16[128,128]{1,0:T(8,128)(2,1)} %param.18) | copy-start | bytes 98308
  48.6 8.3 %copy-start.4 = (bf16[128,128]{1,0:T(8,128)(2,1)S(1)}, bf16[128,128]{1,0:T(8,128)(2,1)}, u32[]{:S(2)}) copy-start(bf16[128,128]{1,0:T(8,128)(2,1)} %param.20) | copy-start | bytes 98308
  48.6 9.0 %copy-start.5 = (bf16[128,128]{1,0:T(8,128)(2,1)S(1)}, bf16[128,128]{1,0:T(8,128)(2,1)}, u32[]{:S(2)}) copy-start(bf16[128,128]{1,0:T(8,128)(2,1)} %param.21) | copy-start | bytes 98308
  48.6 9.1 %copy-start.7 = (f32[128]{0:T(128)S(1)}, f32[128]{0:T(128)}, u32[]{:S(2)}) copy-start(f32[128]{0:T(128)} %param.22) | copy-start | bytes 1540
  48.6 9.9 %copy-start.2 = (f32[48,8,384]{2,1,0:T(8,128)S(1)}, f32[48,8,384]{2,1,0:T(8,128)}, u32[]{:S(2)}) copy-start(f32[48,8,384]{2,1,0:T(8,128)} %get-tuple-element.24) | copy-start | bytes 1769476
  48.6 74.1 %all-to-all-start.2 = ((bf16[32,4,48,128]{3,2,1,0:T(8,128)(2,1)}), bf16[32,4,48,128]{3,2,1,0:T(8,128)(2,1)S(1)}, u32[]{:S(2)}, u32[]{:S(2)}) async-start(bf16[32,4,48,128]{3,2,1,0:T(8,128)(2,1)} %get-tuple-element.25), calls=%async_computation.2 | async-start | bytes 3145728 | tf_op jit(solution)/shard_map/all_to_all | solution.py:334
  56.1 66.0 %copy-start.8 = (s32[32]{0:T(128)}, s32[32]{0:T(128)S(1)}, u32[]{:S(2)}) copy-start(s32[32]{0:T(128)S(1)} %get-tuple-element.22.order_ref) | copy-start | bytes 388
  122.8 1.2 copy-start
  124.0 177.2 %all-to-all-start.4 = ((bf16[32,4,48,128]{3,2,1,0:T(8,128)(2,1)}), bf16[32,4,48,128]{3,2,1,0:T(8,128)(2,1)S(1)}, u32[]{:S(2)}, u32[]{:S(2)}) async-start(bf16[32,4,48,128]{3,2,1,0:T(8,128)(2,1)} %get-tuple-element.26), calls=%async_computation.4 | async-start | bytes 3145728 | tf_op jit(solution)/shard_map/all_to_all | solution.py:334
  301.1 1.1 copy-start.1
  302.3 179.7 %all-to-all-start.1 = ((bf16[32,4,48,128]{3,2,1,0:T(8,128)(2,1)}), bf16[32,4,48,128]{3,2,1,0:T(8,128)(2,1)S(1)}, u32[]{:S(2)}, u32[]{:S(2)}) async-start(bf16[32,4,48,128]{3,2,1,0:T(8,128)(2,1)} %attend.3), calls=%async_computation.1 | async-start | bytes 3145728 | tf_op jit(solution)/shard_map/all_to_all | solution.py:348
  482.0 179.7 %all-to-all-start.3 = ((bf16[32,4,48,128]{3,2,1,0:T(8,128)(2,1)}), bf16[32,4,48,128]{3,2,1,0:T(8,128)(2,1)S(1)}, u32[]{:S(2)}, u32[]{:S(2)}) async-start(bf16[32,4,48,128]{3,2,1,0:T(8,128)(2,1)} %attend.4), calls=%async_computation.3 | async-start | bytes 3145728 | tf_op jit(solution)/shard_map/all_to_all | solution.py:348

commit v3 on v1

v3 whole, which is shorter than its diff:
```python
import math

import jax
import jax.numpy as jnp
from jax import lax
from jax.experimental import pallas as pl
from jax.experimental.pallas import tpu as pltpu
from jax.sharding import PartitionSpec as P

HEADS = 4
WIDTH = 32
SPLIT = (4, 5, 3)
UNIT = 16
F32 = jnp.float32
BF16 = jnp.bfloat16


def dot_nt(a, b):
    return lax.dot_general(a, b, (((1,), (1,)), ((), ())), preferred_element_type=F32)


def dot_tn(a, b):
    return lax.dot_general(a, b, (((0,), (0,)), ((), ())), preferred_element_type=F32)


def turned(matrix):
    return jnp.transpose(matrix.astype(F32)).astype(BF16)


def begin_kernel(
    pair_hbm, gain_ref, shift_ref, bias_ref, all_ref, first_ref, later_ref,
    pair_ref, columns, planes, in_sems, own_sems, late_sems, send_sems, recv_sems,
    pair_send, pair_recv, block_send, block_recv,
):
    rows, cols, channels = pair_ref.shape
    owners = first_ref.shape[0]
    own_cols = cols // owners
    row, col = lax.axis_index("row"), lax.axis_index("col")
    core = col % 2
    here = {"x": row % 4, "y": row // 8, "z": col // 2 * 2 + row // 4 % 2}
    mesh_ids = pl.DeviceIdType.MESH

    def device(place, on_core):
        return ((place["y"] * 2 + place["z"] % 2) * 4 + place["x"], place["z"] // 2 * 2 + on_core)

    def moved(axis, by):
        return {**here, axis: (here[axis] + by) % 4}

    part_rows = rows // 3
    loads = []
    for part in range(3):
        at_rows = pl.ds(part * part_rows, part_rows)
        copy = pltpu.make_async_copy(pair_hbm.at[at_rows], pair_ref.at[at_rows], in_sems.at[part])
        copy.start()
        loads.append(copy)
    partner = device(here, 1 - core)
    outside = device(moved("z", 3 + 2 * (here["z"] % 2)), core)
    peers = [((row + step) % owners, col) for step in range(1, owners)]
    barrier = pltpu.get_barrier_semaphore()
    for friend in peers + [partner, outside]:
        pl.semaphore_signal(barrier, inc=1, device_id=friend, device_id_type=mesh_ids)

    orders = ("zyx", "xzy", "yxz")
    every, low, high = slice(None), pl.ds(0, 2), pl.ds(2, 2)

    def region(part, stage, by, heads):
        place = {}
        for axis in "xyz":
            at = orders[part].index(axis)
            place[axis] = None if at < stage else (here[axis] + by) % 4 if at == stage else here[axis]
        pick = lambda value: slice(None) if value is None else value
        z = place["z"]
        z_hi, z_lo = (None, None) if z is None else (z // 2, z % 2)
        index = (pick(z_hi), core, pick(place["x"]), pick(place["y"]), pick(z_lo), heads)
        return all_ref.at[(*index, pl.ds(part * part_rows, part_rows))]

    def remote(src, dst, sends, recvs, to):
        copy = pltpu.make_async_remote_copy(
            src_ref=src, dst_ref=dst, send_sem=sends, recv_sem=recvs, device_id=to, device_id_type=mesh_ids
        )
        copy.start()
        return copy

    def send(part, stage, kind, by, heads, to):
        ref = region(part, stage, by, heads)
        src = planes.at[:, pl.ds(part * part_rows, part_rows)] if stage == 0 and kind < 2 else ref
        sems = (send_sems.at[part, stage, kind], recv_sems.at[part, stage, kind])
        return remote(src, ref, *sems, device(moved(orders[part][stage], to), core))

    def pair(part, piece, by):
        ref = region(part, 2, by, every)
        return remote(ref, ref, pair_send.at[part, piece], pair_recv.at[part, piece], partner)

    gain, shift = gain_ref[...], shift_ref[...]
    to_planes = turned(jnp.concatenate([bias_ref[...], jnp.zeros((channels, channels - HEADS), BF16)], axis=1))[:8]
    width = 128
    mine, near = [], []
    for part in range(3):
        at_rows = slice(part * part_rows, (part + 1) * part_rows)
        loads[part].wait()

        @pl.loop(0, cols // width)
        def _(chunk):
            at_cols = pl.ds(pl.multiple_of(chunk * width, width), width)
            values = pair_ref[at_rows, at_cols, :].astype(F32)
            centered = values - jnp.mean(values, axis=-1, keepdims=True)
            variance = jnp.mean(centered * centered, axis=-1, keepdims=True)
            normed = centered * lax.rsqrt(variance + 1e-05) * gain + shift
            columns[at_cols, at_rows, :] = jnp.swapaxes(normed, 0, 1).astype(BF16)
            flat = normed.astype(BF16).reshape(part_rows * width, channels)
            by_row = dot_nt(to_planes, flat)
            stacked = jnp.stack([by_row[:, r * width : (r + 1) * width] for r in range(part_rows)], axis=0)
            planes[:, at_rows, at_cols] = jnp.swapaxes(stacked, 0, 1)[:HEADS].astype(BF16)

        if part == 0:
            pl.semaphore_wait(barrier, len(peers) + 2)
        copy = pltpu.make_async_copy(planes.at[:, at_rows], region(part, 0, 0, every), own_sems.at[part])
        copy.start()
        mine.append(copy)
        near.append((send(part, 0, 0, 0, every, 1), send(part, 0, 1, 0, every, 3)))

    first_cols = first_ref.shape[1]
    blocks = []
    for step in range(1, owners):
        to = (row + step) % owners
        src = columns.at[pl.ds(to * own_cols, first_cols)]
        blocks.append(remote(src, first_ref.at[row], block_send.at[step], block_recv.at[step], (to, col)))
    copy = pltpu.make_async_copy(
        columns.at[pl.ds(row * own_cols, first_cols)], first_ref.at[row], own_sems.at[3]
    )
    copy.start()
    mine.append(copy)
    for owner in range(owners):
        src = columns.at[pl.ds(owner * own_cols + first_cols, own_cols - first_cols)]
        copy = pltpu.make_async_copy(src, later_ref.at[owner], late_sems.at[owner])
        copy.start()
        mine.append(copy)
    for copy in mine[:3]:
        copy.wait()

    copies, pairs = [], []
    for stage in range(3):
        last = stage == 2
        if stage:
            near = []
            for part in range(3):
                near.append((send(part, stage, 0, 0, every, 1), send(part, stage, 1, 0, every, 3)))
                if last:
                    pairs.append(pair(part, 0, 0))
        far = []
        for part in range(3):
            near[part][0].wait_recv()
            near[part][1].wait_recv()
            far.append((send(part, stage, 2, 3, low, 1), send(part, stage, 3, 1, high, 3)))
            if last:
                pairs += [pair(part, 1, 3), pair(part, 2, 1)]
        for part in range(3):
            far[part][0].wait_recv()
            far[part][1].wait_recv()
            if last:
                pairs.append(pair(part, 3, 2))
        copies += [copy for two in near + far for copy in two]
    for copy in copies:
        copy.wait_send()
    for copy in pairs + blocks + mine[3:]:
        copy.wait()


def begin(pair_map, ln_gain, ln_bias, w_bias, owners):
    rows, cols, channels = pair_map.shape
    counts = (SPLIT[0], sum(SPLIT[1:]))
    groups = [jax.ShapeDtypeStruct((owners, count, rows, channels), BF16) for count in counts]
    planes = jax.ShapeDtypeStruct((2, 2, 4, 4, 2, HEADS, rows, cols), BF16)
    vmem, anywhere = pl.BlockSpec(memory_space=pltpu.VMEM), pl.BlockSpec(memory_space=pl.ANY)
    dma = pltpu.SemaphoreType.DMA
    return pl.pallas_call(
        begin_kernel,
        in_specs=[anywhere] + [vmem] * 3,
        out_specs=[anywhere] * 3,
        out_shape=[planes] + groups,
        scratch_shapes=[
            pltpu.VMEM((rows, cols, channels), BF16),
            pltpu.VMEM((cols, rows, channels), BF16),
            pltpu.VMEM((HEADS, rows, cols), BF16),
            dma((3,)),
            dma((4,)),
            dma((owners,)),
            dma((3, 3, 4)),
            dma((3, 3, 4)),
            dma((3, 4)),
            dma((3, 4)),
            dma((owners,)),
            dma((owners,)),
        ],
        compiler_params=pltpu.CompilerParams(
            collective_id=0, has_side_effects=True, vmem_limit_bytes=60 * 2**20
        ),
        name="begin",
    )(pair_map, ln_gain[None], ln_bias[None], w_bias)


def give_back_kernel(mine_ref, got_ref, own_sem, sends, recvs):
    owners = mine_ref.shape[0]
    row, col = lax.axis_index("row"), lax.axis_index("col")
    barrier = pltpu.get_barrier_semaphore()
    peers = [(row + step) % owners for step in range(1, owners)]
    for peer in peers:
        pl.semaphore_signal(barrier, inc=1, device_id=(peer, col), device_id_type=pl.DeviceIdType.MESH)
    own = pltpu.make_async_copy(mine_ref.at[row], got_ref.at[row], own_sem)
    own.start()
    pl.semaphore_wait(barrier, len(peers))
    copies = []
    for step, peer in enumerate(peers):
        copy = pltpu.make_async_remote_copy(
            src_ref=mine_ref.at[peer],
            dst_ref=got_ref.at[row],
            send_sem=sends.at[step],
            recv_sem=recvs.at[step],
            device_id=(peer, col),
            device_id_type=pl.DeviceIdType.MESH,
        )
        copy.start()
        copies.append(copy)
    own.wait()
    for copy in copies:
        copy.wait()


def give_back(update):
    owners = update.shape[0]
    return pl.pallas_call(
        give_back_kernel,
        in_specs=[pl.BlockSpec(memory_space=pl.ANY)],
        out_specs=pl.BlockSpec(memory_space=pl.ANY),
        out_shape=jax.ShapeDtypeStruct(update.shape, BF16),
        scratch_shapes=[
            pltpu.SemaphoreType.DMA,
            pltpu.SemaphoreType.DMA((owners - 1,)),
            pltpu.SemaphoreType.DMA((owners - 1,)),
        ],
        compiler_params=pltpu.CompilerParams(collective_id=1, has_side_effects=True),
        name="give_back",
    )(update)


def attend_kernel(
    tokens_ref, x_ref, planes_ref, real_ref, wq_ref, wk_ref, wv_ref, wg_ref, gate_bias_ref, wo_ref,
    out_ref, bias, keys, values, queries, summed, real, wqg, wv, gate_bias, order, sems,
):
    owners, _, rows, channels = x_ref.shape
    length = owners * rows
    units, per_owner = length // UNIT, rows // UNIT
    chain_units = units // 4
    first = pl.program_id(0) == 0

    def filled(chain):
        def count(unit, total):
            return total + tokens_ref[(chain * chain_units + unit) * UNIT]

        return lax.fori_loop(0, chain_units, count, jnp.int32(0))

    @pl.when(first)
    def _():
        ends = jnp.int32(0)
        for chain in range(4):
            here = filled(chain)

            def note(unit, start, chain=chain):
                order[start + unit] = chain * chain_units + unit
                return start

            lax.fori_loop(0, here, note, ends)
            ends = ends + here
        order[units] = ends

        @pl.loop(ends, units)
        def _(unit):
            order[unit] = 0

    count = order[units]
    tiles = (count + 7) // 8

    def plane_copy(slot):
        unit = order[slot]
        owner = unit // per_owner
        at = pl.ds(pl.multiple_of(unit % per_owner * UNIT, UNIT), UNIT)
        to = pl.ds(pl.multiple_of(slot * UNIT, UNIT), UNIT)
        return pltpu.make_async_copy(
            planes_ref.at[:, :, owner % 4, owner // 8, owner // 4 % 2, :, at, :],
            bias.at[:, :, :, to, :],
            sems.at[slot // 16],
        )

    @pl.when(first)
    def _():
        @pl.loop(0, tiles * 8)
        def _(slot):
            plane_copy(slot).start()

        for slot in range(units):
            unit = order[slot]
            at = pl.ds(pl.multiple_of(unit * UNIT, UNIT), UNIT)
            keep = jnp.where(slot < count, 1.0, 0.0).astype(F32)
            real[slot * UNIT : (slot + 1) * UNIT, :] = (real_ref[at, :].astype(F32) * keep).astype(BF16)
        wqg[:channels] = turned(wq_ref[...])
        wqg[channels:] = turned(wg_ref[...])
        wv[...] = turned(wv_ref[...])
        gate_bias[...] = jnp.transpose(jnp.broadcast_to(gate_bias_ref[...], (channels, channels)))

    x = x_ref[...].reshape(length, channels)
    projected = dot_nt(wqg[...], x)
    queries[...] = (projected[:channels] * (1.0 / math.sqrt(WIDTH))).astype(BF16)
    gate = jax.nn.sigmoid(projected[channels:] + gate_bias[:, :1])
    pieces = []
    for slot in range(units):
        unit = order[slot]
        at = pl.ds(pl.multiple_of(unit % per_owner * UNIT, UNIT), UNIT)
        pieces.append(x_ref[unit // per_owner, 0, at, :])
    compact = jnp.concatenate(pieces, axis=0) * real[...]
    key_all = jnp.dot(compact, wk_ref[...], preferred_element_type=F32).astype(BF16)
    value_all = dot_nt(wv[...], compact).astype(BF16)
    ones = dot_nt(jnp.full((16, channels), 1.0 / channels, BF16), real[...]).astype(BF16)
    for head in range(HEADS):
        lanes = slice(head * WIDTH, (head + 1) * WIDTH)
        keys[head] = key_all[:, lanes]
        values[head, :WIDTH] = value_all[lanes]
        values[head, WIDTH:] = ones

    def arrived(start, count):
        @pl.when(first)
        def _():
            @pl.loop(start, start + count)
            def _(slot):
                plane_copy(slot).wait()

    def scores(head, at):
        heads = pl.ds(head * WIDTH, WIDTH)
        raw = jnp.dot(keys[head, at, :], queries[heads, :], preferred_element_type=F32)
        added = [bias[z, core, head, at, :] for z in range(2) for core in range(2)]
        return raw + jnp.concatenate(added, axis=1).astype(F32)

    summed[...] = jnp.zeros_like(summed)

    def advance(at):
        for head in range(HEADS):
            weights = jnp.exp(scores(head, at)).astype(BF16)
            summed[head] += jnp.dot(values[head, :, at], weights, preferred_element_type=F32)

    wide = tiles // 2

    @pl.loop(0, wide)
    def _(step):
        arrived(step * 16, 16)
        advance(pl.ds(pl.multiple_of(step * 256, 256), 256))

    @pl.when(tiles % 2 == 1)
    def _():
        arrived(wide * 16, 8)
        advance(pl.ds(pl.multiple_of(wide * 256, 256), 128))

    totals = summed[:, WIDTH, :]
    lowest, highest = jnp.min(totals), jnp.max(totals)
    safe = jnp.logical_and(lowest > 2.0**-60, highest < 2.0**100)

    @pl.when(jnp.logical_not(safe))
    def _():
        for head in range(HEADS):

            def masked(step):
                at = pl.ds(pl.multiple_of(step * 128, 128), 128)
                return at, jnp.where(real[at, :1].astype(F32) > 0, scores(head, at), -3.0e38)

            def highest_of(step, top):
                return jnp.maximum(top, jnp.max(masked(step)[1], axis=0, keepdims=True))

            top = lax.fori_loop(0, tiles, highest_of, jnp.full((1, length), -3.0e38, F32))
            summed[head] = jnp.zeros_like(summed[head])

            @pl.loop(0, tiles)
            def _(step):
                at, shifted = masked(step)
                weights = jnp.exp(shifted - top).astype(BF16)
                summed[head] += jnp.dot(values[head, :, at], weights, preferred_element_type=F32)

    attended = jnp.concatenate(
        [summed[head, :WIDTH] / summed[head, WIDTH : WIDTH + 1] for head in range(HEADS)], axis=0
    )
    hidden = (gate * attended).astype(BF16)
    update = dot_tn(hidden, wo_ref[...]).astype(BF16)
    out_ref[...] = update.reshape(out_ref.shape)


def attend(x, start, cols, planes, tokens, real, wq, wk, wv, wg, gate_bias, wo):
    owners, _, rows, channels = x.shape
    length = owners * rows
    whole = lambda shape: pl.BlockSpec(shape, lambda j, *_: (0,) * len(shape))
    column = pl.BlockSpec((owners, 1, rows, channels), lambda j, *_: (0, j + start, 0, 0))
    result = pl.BlockSpec((owners, 1, rows, channels), lambda j, *_: (0, j, 0, 0))
    scores = cols * HEADS * length * length
    return pl.pallas_call(
        attend_kernel,
        grid_spec=pltpu.PrefetchScalarGridSpec(
            num_scalar_prefetch=1,
            grid=(cols,),
            in_specs=[
                column,
                pl.BlockSpec(memory_space=pl.ANY),
                whole(real.shape),
                whole(wq.shape),
                whole(wk.shape),
                whole(wv.shape),
                whole(wg.shape),
                whole(gate_bias.shape),
                whole(wo.shape),
            ],
            out_specs=result,
            scratch_shapes=[
                pltpu.VMEM((2, 2, HEADS, length, length // 4), BF16),
                pltpu.VMEM((HEADS, length, WIDTH), BF16),
                pltpu.VMEM((HEADS, WIDTH + 16, length), BF16),
                pltpu.VMEM((channels, length), BF16),
                pltpu.VMEM((HEADS, WIDTH + 16, length), F32),
                pltpu.VMEM((length, channels), BF16),
                pltpu.VMEM((2 * channels, channels), BF16),
                pltpu.VMEM((channels, channels), BF16),
                pltpu.VMEM((channels, channels), F32),
                pltpu.SMEM((length // UNIT + 1,), jnp.int32),
                pltpu.SemaphoreType.DMA((length // (16 * UNIT),)),
            ],
        ),
        out_shape=jax.ShapeDtypeStruct((owners, cols, rows, channels), BF16),
        compiler_params=pltpu.CompilerParams(vmem_limit_bytes=60 * 2**20),
        cost_estimate=pl.CostEstimate(
            flops=scores * 2048, bytes_accessed=planes.size * 2 + x.size * 4, transcendentals=scores
        ),
        name="attend",
    )(tokens, x, planes, real, wq, wk, wv, wg, gate_bias, wo)


def shards(
    pair_map, valid_tokens, ln_gain, ln_bias, w_bias, w_query, w_key, w_value, w_gate, gate_bias, w_out,
):
    rows, cols, channels = pair_map.shape
    owners = lax.axis_size("row")
    length = valid_tokens.shape[0]
    planes, first, later = begin(pair_map, ln_gain, ln_bias, w_bias, owners)
    later = lax.all_to_all(later, "row", split_axis=0, concat_axis=0)
    real = jnp.broadcast_to(valid_tokens[:, None], (length, channels)).astype(BF16)
    arguments = (planes, valid_tokens, real, w_query, w_key, w_value, w_gate, gate_bias[None], w_out)
    returned = []
    source, start = first, 0
    for index, count in enumerate(SPLIT):
        update = attend(source, start, count, *arguments)
        start = start + count if index else 0
        source = later
        if index < len(SPLIT) - 1:
            returned.append(lax.all_to_all(update, "row", split_axis=0, concat_axis=0))
        else:
            returned.append(give_back(update))
    update = jnp.concatenate(returned, axis=1).reshape(cols, rows, channels)
    return jnp.swapaxes(update, 0, 1)


def solution(mesh):
    return jax.shard_map(
        shards,
        mesh=mesh,
        in_specs=(P("row", "col", None), P(), P(), P(), P(), P(), P(), P(), P(), P(), P()),
        out_specs=P("row", "col", None),
        check_vma=False,
    )
```

time: 784 us -> 613 us (0.78)
  starting transfers between devices: 207 us -> 21.7 us
  Pallas kernels: 449 us -> 583 us
  blocking collectives: 83.6 us -> 0 us
  waiting for transfers between devices: 14.5 us -> 0.01 us
  between operations: 14.3 us -> 0.12 us
    all_to_all x2 -> x1, starting transfers between devices: 190 us -> 4.91 us  [shards(): later = lax.all_to_all(later, 'row', split_axis=0, concat_axis=0)]
    pallas_call x1 -> x2, Pallas kernels: 15.6 us -> 103 us  [the longest x1 81.2 us: begin(): pl.pallas_call(begin_kernel, in_specs=[anywhere] + [vmem] * 3, out_specs=...]
    all_to_all x2 -> x0, blocking collectives: 73.2 us -> none  [the longest x1 46.5 us: shards(): lax.all_to_all(group, 'row', split_axis=0, concat_axis=0)]
    pallas_call x3, Pallas kernels: 433 us -> 480 us  [attend(): pl.pallas_call(attend_kernel, grid_spec=pltpu.PrefetchScalarGridSpec(num_...]
    all_to_all x2 -> x1, waiting for transfers between devices: 14.5 us -> 0.01 us  [shards(): later = lax.all_to_all(later, 'row', split_axis=0, concat_axis=0)]
    all_gather x1 -> x0, blocking collectives: 10.4 us -> none  [shards(): planes = lax.all_gather(planes, 'col')]
  transfers between devices with their start and end apart: 5 -> 3, of which waited for: 1 -> 0; matrix products, arithmetic and copies ran while one was open for 1% -> 0% of each run, Pallas kernels for 55% -> 82%
where the time goes in v3:
time: 613 us
  Pallas kernels  583 us (95%)
  starting transfers between devices  21.7 us (4%)
    pallas_call x3, Pallas kernels, attend(): pl.pallas_call(attend_kernel, grid_spec=pltpu.PrefetchScalarGridSpec(num_...  480 us
    pallas_call x1, Pallas kernels, begin(): pl.pallas_call(begin_kernel, in_specs=[anywhere] + [vmem] * 3, out_specs=...  81.2 us
    pallas_call x1, Pallas kernels, give_back(): pl.pallas_call(give_back_kernel, in_specs=[pl.BlockSpec(memory_space=pl.A...  22.2 us
    all_to_all x2, starting transfers between devices, shards(): returned.append(lax.all_to_all(update, 'row', split_axis=0, concat_axis=0))  16.7 us
  transfers between devices with their start and end apart: 3, of which 0 were waited for; matrix products, arithmetic and copies ran while one was open for 0% of the time, Pallas kernels for 82%

profile of v3, /device:TPU:0, one launch (start us, length us, event | category | flops | bytes accessed | tf_op | source)
XLA Modules:
  0.0 612.7 jit_solution(5750108476928863419)
XLA Ops:
  0.0 1.4 copy.12.bias_ref
  1.4 81.2 %begin.1 = (bf16[2,2,4,4,2,4,48,384]{7,6,5,4,3,2,1,0:T(8,128)(2,1)}, bf16[32,4,48,128]{3,2,1,0:T(8,128)(2,1)}, bf16[32,8,48,128]{3,2,1,0:T(8,128)(2,1)}) custom-call(bf16[48,384,128]{2,1,0:T(8,128)(2,1)} %pair_hbm.1, f32[1,128]{1,0:T(1,128)} %bitcast.8, f32[1,128]{1,0:T(1,128)} %bitcast.9, bf16[128,4]{1,0:T(8,128)(2,1)} %copy.12.bias_ref), custom_call_target="tpu_custom_call" | custom-call | tf_op jit(solution)/shard_map/begin/pallas_call | solution.py:176
  82.6 0.0 copy-start
  82.7 4.9 all-to-all-start.1
  87.6 0.0 copy-done
  87.6 1.0 broadcast_in_dim.17.real_ref
  88.6 160.0 %attend.3 = bf16[32,4,48,128]{3,2,1,0:T(8,128)(2,1)} custom-call(s32[1536]{0:T(1024)} %tokens_ref.5, bf16[32,4,48,128]{3,2,1,0:T(8,128)(2,1)} %get-tuple-element.8.x_ref, bf16[2,2,4,4,2,4,48,384]{7,6,5,4,3,2,1,0:T(8,128)(2,1)} %get-tuple-element.9.planes_ref, bf16[1536,128]{1,0:T(8,128)(2,1)} %broadcast_in_dim.17.real_ref, bf16[128,128]{1,0:T(8,128)(2,1)} %wq_ref.5, ...), custom_call_target="tpu_custom_call" | custom-call | flops 77309411328 | bytes 22020096 | tf_op jit(solution)/shard_map/attend/pallas_call | solution.py:400
  248.6 0.0 all-to-all-done.1.x_ref
  248.6 8.4 %all-to-all-start = ((bf16[32,4,48,128]{3,2,1,0:T(8,128)(2,1)}), bf16[32,4,48,128]{3,2,1,0:T(8,128)(2,1)S(1)}, u32[]{:S(2)}, u32[]{:S(2)}) async-start(bf16[32,4,48,128]{3,2,1,0:T(8,128)(2,1)} %attend.3), calls=%async_computation | async-start | bytes 3145728 | tf_op jit(solution)/shard_map/all_to_all | solution.py:457
  257.0 198.4 %attend.4 = bf16[32,5,48,128]{3,2,1,0:T(8,128)(2,1)} custom-call(s32[1536]{0:T(1024)} %tokens_ref.5, bf16[32,8,48,128]{3,2,1,0:T(8,128)(2,1)} %all-to-all-done.1.x_ref, bf16[2,2,4,4,2,4,48,384]{7,6,5,4,3,2,1,0:T(8,128)(2,1)} %get-tuple-element.9.planes_ref, bf16[1536,128]{1,0:T(8,128)(2,1)} %broadcast_in_dim.17.real_ref, bf16[128,128]{1,0:T(8,128)(2,1)} %wq_ref.5, ...), custom_call_target="tpu_custom_call" | custom-call | flops 96636764160 | bytes 25165824 | tf_op jit(solution)/shard_map/attend/pallas_call | solution.py:400
  455.4 0.0 all-to-all-done
  455.4 8.3 %all-to-all-start.2 = ((bf16[32,5,48,128]{3,2,1,0:T(8,128)(2,1)}), bf16[32,5,48,128]{3,2,1,0:T(8,128)(2,1)S(1)}, u32[]{:S(2)}, u32[]{:S(2)}) async-start(bf16[32,5,48,128]{3,2,1,0:T(8,128)(2,1)} %attend.4), calls=%async_computation.2 | async-start | bytes 3932160 | tf_op jit(solution)/shard_map/all_to_all | solution.py:457
  463.7 121.7 %attend.5.mine_ref = bf16[32,3,48,128]{3,2,1,0:T(8,128)(2,1)} custom-call(s32[1536]{0:T(1024)} %tokens_ref.5, bf16[32,8,48,128]{3,2,1,0:T(8,128)(2,1)} %all-to-all-done.1.x_ref, bf16[2,2,4,4,2,4,48,384]{7,6,5,4,3,2,1,0:T(8,128)(2,1)} %get-tuple-element.9.planes_ref, bf16[1536,128]{1,0:T(8,128)(2,1)} %broadcast_in_dim.17.real_ref, bf16[128,128]{1,0:T(8,128)(2,1)} %wq_ref.5, ...), custom_call_target="tpu_custom_call" | custom-call | flops 57982058496 | bytes 25165824 | tf_op jit(solution)/shard_map/attend/pallas_call | solution.py:400
  585.4 22.2 %give_back.1 = bf16[32,3,48,128]{3,2,1,0:T(8,128)(2,1)} custom-call(bf16[32,3,48,128]{3,2,1,0:T(8,128)(2,1)} %attend.5.mine_ref), custom_call_target="tpu_custom_call" | custom-call | tf_op jit(solution)/shard_map/give_back/pallas_call | solution.py:231
  607.6 0.0 all-to-all-done.2
  607.6 1.6 pad_maximum_fusion
  609.3 3.4 copy.15
  (1 shorter events, 0.0 us)
Async XLA Ops:
  82.6 4.9 copy-start
  82.7 165.9 %all-to-all-start.1 = ((bf16[32,8,48,128]{3,2,1,0:T(8,128)(2,1)}), bf16[32,8,48,128]{3,2,1,0:T(8,128)(2,1)}, u32[]{:S(2)}, u32[]{:S(2)}) async-start(bf16[32,8,48,128]{3,2,1,0:T(8,128)(2,1)} %get-tuple-element.10), calls=%async_computation.1 | async-start | bytes 6291456 | tf_op jit(solution)/shard_map/all_to_all | solution.py:447
  248.6 206.8 %all-to-all-start = ((bf16[32,4,48,128]{3,2,1,0:T(8,128)(2,1)}), bf16[32,4,48,128]{3,2,1,0:T(8,128)(2,1)S(1)}, u32[]{:S(2)}, u32[]{:S(2)}) async-start(bf16[32,4,48,128]{3,2,1,0:T(8,128)(2,1)} %attend.3), calls=%async_computation | async-start | bytes 3145728 | tf_op jit(solution)/shard_map/all_to_all | solution.py:457
  455.4 152.2 %all-to-all-start.2 = ((bf16[32,5,48,128]{3,2,1,0:T(8,128)(2,1)}), bf16[32,5,48,128]{3,2,1,0:T(8,128)(2,1)S(1)}, u32[]{:S(2)}, u32[]{:S(2)}) async-start(bf16[32,5,48,128]{3,2,1,0:T(8,128)(2,1)} %attend.4), calls=%async_computation.2 | async-start | bytes 3932160 | tf_op jit(solution)/shard_map/all_to_all | solution.py:457

commit v4 on v3

--- a/solution.py
+++ b/solution.py
@@ -333,30 +333,51 @@
             def _(slot):
                 plane_copy(slot).wait()
 
-    def scores(head, at):
+    part_width = length // 4
+
+    def scores(head, at, low, high):
         heads = pl.ds(head * WIDTH, WIDTH)
-        raw = jnp.dot(keys[head, at, :], queries[heads, :], preferred_element_type=F32)
-        added = [bias[z, core, head, at, :] for z in range(2) for core in range(2)]
+        raw = jnp.dot(keys[head, at, :], queries[heads, low:high], preferred_element_type=F32)
+        added = []
+        for part in range(4):
+            start, end = max(low - part * part_width, 0), min(high - part * part_width, part_width)
+            if start < end:
+                added.append(bias[part // 2, part % 2, head, at, start:end])
         return raw + jnp.concatenate(added, axis=1).astype(F32)
 
     summed[...] = jnp.zeros_like(summed)
 
-    def advance(at):
-        for head in range(HEADS):
-            weights = jnp.exp(scores(head, at)).astype(BF16)
-            summed[head] += jnp.dot(values[head, :, at], weights, preferred_element_type=F32)
+    def advance(at, width):
+        def add(head, low, weights):
+            summed[head, :, low : low + width] += jnp.dot(
+                values[head, :, at], weights, preferred_element_type=F32
+            )
+
+        pieces = [(head, low) for head in range(HEADS) for low in range(0, length, width)]
+        scored, weighted = None, None
+        for piece in pieces + [None, None]:
+            coming = None
+            if piece is not None:
+                head, low = piece
+                coming = (head, low, scores(head, at, low, low + width))
+            ready = None
+            if scored is not None:
+                ready = (*scored[:2], jnp.exp(scored[2]).astype(BF16))
+            if weighted is not None:
+                add(*weighted)
+            scored, weighted = coming, ready
 
     wide = tiles // 2
 
     @pl.loop(0, wide)
     def _(step):
         arrived(step * 16, 16)
-        advance(pl.ds(pl.multiple_of(step * 256, 256), 256))
+        advance(pl.ds(pl.multiple_of(step * 256, 256), 256), 512)
 
     @pl.when(tiles % 2 == 1)
     def _():
         arrived(wide * 16, 8)
-        advance(pl.ds(pl.multiple_of(wide * 256, 256), 128))
+        advance(pl.ds(pl.multiple_of(wide * 256, 256), 128), 768)
 
     totals = summed[:, WIDTH, :]
     lowest, highest = jnp.min(totals), jnp.max(totals)
@@ -368,7 +389,7 @@
 
             def masked(step):
                 at = pl.ds(pl.multiple_of(step * 128, 128), 128)
-                return at, jnp.where(real[at, :1].astype(F32) > 0, scores(head, at), -3.0e38)
+                return at, jnp.where(real[at, :1].astype(F32) > 0, scores(head, at, 0, length), -3.0e38)
 
             def highest_of(step, top):
                 return jnp.maximum(top, jnp.max(masked(step)[1], axis=0, keepdims=True))

time: 613 us -> 588 us (0.959)
  Pallas kernels: 583 us -> 558 us
    pallas_call x3, Pallas kernels: 480 us -> 455 us  [attend(): pl.pallas_call(attend_kernel, grid_spec=pltpu.PrefetchScalarGridSpec(num_...]
  transfers between devices with their start and end apart: 3 -> 3, of which waited for: 0 -> 0; matrix products, arithmetic and copies ran while one was open for 0% -> 0% of each run, Pallas kernels for 82% -> 81%
where the time goes in v4:
time: 588 us; the launch traced here: 587 us
  Pallas kernels  558 us (95%)
  starting transfers between devices  21.7 us (4%)
    pallas_call x3, Pallas kernels, attend(): pl.pallas_call(attend_kernel, grid_spec=pltpu.PrefetchScalarGridSpec(num_...  455 us
    pallas_call x1, Pallas kernels, begin(): pl.pallas_call(begin_kernel, in_specs=[anywhere] + [vmem] * 3, out_specs=...  81.2 us
    pallas_call x1, Pallas kernels, give_back(): pl.pallas_call(give_back_kernel, in_specs=[pl.BlockSpec(memory_space=pl.A...  21.9 us
    all_to_all x2, starting transfers between devices, shards(): returned.append(lax.all_to_all(update, 'row', split_axis=0, concat_axis=0))  16.8 us
  transfers between devices with their start and end apart: 3, of which 0 were waited for; matrix products, arithmetic and copies ran while one was open for 0% of the time, Pallas kernels for 81%

profile of v4, /device:TPU:0, one launch (start us, length us, event | category | flops | bytes accessed | tf_op | source)
XLA Modules:
  0.0 587.0 jit_solution(4287812186041654564)
XLA Ops:
  0.0 1.4 copy.12.bias_ref
  1.4 81.2 %begin.1 = (bf16[2,2,4,4,2,4,48,384]{7,6,5,4,3,2,1,0:T(8,128)(2,1)}, bf16[32,4,48,128]{3,2,1,0:T(8,128)(2,1)}, bf16[32,8,48,128]{3,2,1,0:T(8,128)(2,1)}) custom-call(bf16[48,384,128]{2,1,0:T(8,128)(2,1)} %pair_hbm.1, f32[1,128]{1,0:T(1,128)} %bitcast.8, f32[1,128]{1,0:T(1,128)} %bitcast.9, bf16[128,4]{1,0:T(8,128)(2,1)} %copy.12.bias_ref), custom_call_target="tpu_custom_call" | custom-call | tf_op jit(solution)/shard_map/begin/pallas_call | solution.py:176
  82.6 0.0 copy-start
  82.7 4.9 all-to-all-start.1
  87.6 0.0 copy-done
  87.6 1.0 broadcast_in_dim.17.real_ref
  88.6 151.5 %attend.3 = bf16[32,4,48,128]{3,2,1,0:T(8,128)(2,1)} custom-call(s32[1536]{0:T(1024)} %tokens_ref.5, bf16[32,4,48,128]{3,2,1,0:T(8,128)(2,1)} %get-tuple-element.8.x_ref, bf16[2,2,4,4,2,4,48,384]{7,6,5,4,3,2,1,0:T(8,128)(2,1)} %get-tuple-element.9.planes_ref, bf16[1536,128]{1,0:T(8,128)(2,1)} %broadcast_in_dim.17.real_ref, bf16[128,128]{1,0:T(8,128)(2,1)} %wq_ref.5, ...), custom_call_target="tpu_custom_call" | custom-call | flops 77309411328 | bytes 22020096 | tf_op jit(solution)/shard_map/attend/pallas_call | solution.py:421
  240.1 0.0 all-to-all-done.1.x_ref
  240.1 8.5 %all-to-all-start = ((bf16[32,4,48,128]{3,2,1,0:T(8,128)(2,1)}), bf16[32,4,48,128]{3,2,1,0:T(8,128)(2,1)S(1)}, u32[]{:S(2)}, u32[]{:S(2)}) async-start(bf16[32,4,48,128]{3,2,1,0:T(8,128)(2,1)} %attend.3), calls=%async_computation | async-start | bytes 3145728 | tf_op jit(solution)/shard_map/all_to_all | solution.py:478
  248.6 187.8 %attend.4 = bf16[32,5,48,128]{3,2,1,0:T(8,128)(2,1)} custom-call(s32[1536]{0:T(1024)} %tokens_ref.5, bf16[32,8,48,128]{3,2,1,0:T(8,128)(2,1)} %all-to-all-done.1.x_ref, bf16[2,2,4,4,2,4,48,384]{7,6,5,4,3,2,1,0:T(8,128)(2,1)} %get-tuple-element.9.planes_ref, bf16[1536,128]{1,0:T(8,128)(2,1)} %broadcast_in_dim.17.real_ref, bf16[128,128]{1,0:T(8,128)(2,1)} %wq_ref.5, ...), custom_call_target="tpu_custom_call" | custom-call | flops 96636764160 | bytes 25165824 | tf_op jit(solution)/shard_map/attend/pallas_call | solution.py:421
  436.4 0.0 all-to-all-done
  436.4 8.4 %all-to-all-start.2 = ((bf16[32,5,48,128]{3,2,1,0:T(8,128)(2,1)}), bf16[32,5,48,128]{3,2,1,0:T(8,128)(2,1)S(1)}, u32[]{:S(2)}, u32[]{:S(2)}) async-start(bf16[32,5,48,128]{3,2,1,0:T(8,128)(2,1)} %attend.4), calls=%async_computation.2 | async-start | bytes 3932160 | tf_op jit(solution)/shard_map/all_to_all | solution.py:478
  444.8 115.2 %attend.5.mine_ref = bf16[32,3,48,128]{3,2,1,0:T(8,128)(2,1)} custom-call(s32[1536]{0:T(1024)} %tokens_ref.5, bf16[32,8,48,128]{3,2,1,0:T(8,128)(2,1)} %all-to-all-done.1.x_ref, bf16[2,2,4,4,2,4,48,384]{7,6,5,4,3,2,1,0:T(8,128)(2,1)} %get-tuple-element.9.planes_ref, bf16[1536,128]{1,0:T(8,128)(2,1)} %broadcast_in_dim.17.real_ref, bf16[128,128]{1,0:T(8,128)(2,1)} %wq_ref.5, ...), custom_call_target="tpu_custom_call" | custom-call | flops 57982058496 | bytes 25165824 | tf_op jit(solution)/shard_map/attend/pallas_call | solution.py:421
  560.0 21.9 %give_back.1 = bf16[32,3,48,128]{3,2,1,0:T(8,128)(2,1)} custom-call(bf16[32,3,48,128]{3,2,1,0:T(8,128)(2,1)} %attend.5.mine_ref), custom_call_target="tpu_custom_call" | custom-call | tf_op jit(solution)/shard_map/give_back/pallas_call | solution.py:231
  582.0 0.0 all-to-all-done.2
  582.0 1.6 pad_maximum_fusion
  583.6 3.4 copy.15
  (1 shorter events, 0.0 us)
Async XLA Ops:
  82.6 4.9 copy-start
  82.7 157.5 %all-to-all-start.1 = ((bf16[32,8,48,128]{3,2,1,0:T(8,128)(2,1)}), bf16[32,8,48,128]{3,2,1,0:T(8,128)(2,1)}, u32[]{:S(2)}, u32[]{:S(2)}) async-start(bf16[32,8,48,128]{3,2,1,0:T(8,128)(2,1)} %get-tuple-element.10), calls=%async_computation.1 | async-start | bytes 6291456 | tf_op jit(solution)/shard_map/all_to_all | solution.py:468
  240.1 196.3 %all-to-all-start = ((bf16[32,4,48,128]{3,2,1,0:T(8,128)(2,1)}), bf16[32,4,48,128]{3,2,1,0:T(8,128)(2,1)S(1)}, u32[]{:S(2)}, u32[]{:S(2)}) async-start(bf16[32,4,48,128]{3,2,1,0:T(8,128)(2,1)} %attend.3), calls=%async_computation | async-start | bytes 3145728 | tf_op jit(solution)/shard_map/all_to_all | solution.py:478
  436.4 145.6 %all-to-all-start.2 = ((bf16[32,5,48,128]{3,2,1,0:T(8,128)(2,1)}), bf16[32,5,48,128]{3,2,1,0:T(8,128)(2,1)S(1)}, u32[]{:S(2)}, u32[]{:S(2)}) async-start(bf16[32,5,48,128]{3,2,1,0:T(8,128)(2,1)} %attend.4), calls=%async_computation.2 | async-start | bytes 3932160 | tf_op jit(solution)/shard_map/all_to_all | solution.py:478
